TPU v7x, 32 devices: a whole 2x2x4 slice. The times are simulated.
32 devices in a mesh: row: 4 (over z), col: 8 (over y, x, core).
Axes of the slice: x: 2, y: 2, z: 4, core: 2. Of those that a mesh axis runs over, the one named last changes fastest.
Arguments:
- point_data: float32 [4, 8192], P(None, ('row', 'col')), may hold values from 0 to 4, as said below
- right_side: float32 [64, 8192], P(None, ('row', 'col')), may hold values from -45 to 45
- pair_list: int32 [2, 468], replicated, may hold values from 0 to 63, as said below
Outputs:
- solution: float32 [64, 8192], P(None, ('row', 'col'))
- residual: float32 [64, 8192], P(None, ('row', 'col'))
Inputs may be any that keep to these rules, and one draw needn't show every extreme that they name: `point_data`: the points of block b lie in one unit cell of a 4 x 4 x 4 grid, one block to a cell; row 3 lies in 0.2 to 0.6. `pair_list`: each column (I, J) has I < J and names two blocks whose cells lie within one cell of each other along every dimension; every such pair is listed exactly once. The columns stand grouped by the device (I // 2 // 8, (J // 2) % 8) of the row and col axes, groups in row-major order.
All inputs are finite; a program needn't handle non-finite values.
Results may differ from a plain program's by a relative error of at most 0.018.
Values may be sent and summed in bfloat16 or wider, within the bound.
No kernel may reach another device: no remote copies, remote signals or barrier semaphores. Data moves between devices by JAX's collectives and lax.ppermute only.
A program may use at most 64 MiB of HBM per device.

v0:
```python
import functools
import jax
import jax.numpy as jnp
from jax import lax
from jax.experimental import pallas as pl
from jax.experimental.pallas import tpu as pltpu
from jax.sharding import PartitionSpec as P

BLOCK = 128
ITERS = 3


long_range = 1.0
short_range = 0.35
nugget = 1.0
tiles_per_step = 8
rows_here = 4
chunk = 4
chunks_per_step = 8
tile_bytes_limit = 24 * 2**20
kernel_bytes = 12 * 2**20
f32 = jnp.float32
bf16 = jnp.bfloat16


def wendland(distance, reach):
    scaled = distance / reach
    remain = jnp.maximum(1.0 - scaled, 0.0)
    square = remain * remain
    return square * square * (4.0 * scaled + 1.0)


def covariance_tiles(row_points, column_points):
    delta_x = row_points[:, 0, :, None] - column_points[:, 0, None, :]
    delta_y = row_points[:, 1, :, None] - column_points[:, 1, None, :]
    delta_z = row_points[:, 2, :, None] - column_points[:, 2, None, :]
    distance = jnp.sqrt(delta_x * delta_x + delta_y * delta_y + delta_z * delta_z)
    kernel = wendland(distance, long_range) + wendland(distance, short_range)
    return row_points[:, 3, :, None] * kernel * column_points[:, 3, None, :]


def as_blocks(points):
    return points.reshape(4, -1, BLOCK).transpose(1, 0, 2)


def by_points(point_data, right_side, pair_list):
    col_devices = lax.axis_size("col")
    my_row = lax.axis_index("row")
    my_column = lax.axis_index("col")
    points = point_data.shape[1]
    blocks_here = points // BLOCK
    realizations = right_side.shape[0]
    own_blocks = as_blocks(point_data)
    row_blocks = as_blocks(lax.all_gather(point_data, "col", axis=1, tiled=True))
    column_blocks = as_blocks(lax.all_gather(point_data, "row", axis=1, tiled=True))
    row_count = row_blocks.shape[0]
    column_count = column_blocks.shape[0]
    lower_block = pair_list[0]
    upper_block = pair_list[1]
    this_device = my_row * col_devices + my_column
    device_of = (
        lower_block // blocks_here // col_devices * col_devices
        + upper_block // blocks_here % col_devices
    )
    roster_first_pair = jnp.sum((device_of < this_device).astype(jnp.int32))
    roster_pair_count = jnp.sum((device_of == this_device).astype(jnp.int32))
    roster_row_slot = jnp.clip(lower_block - my_row * col_devices * blocks_here, 0, row_count - 1)
    roster_column_slot = jnp.clip(
        upper_block // blocks_here // col_devices * blocks_here + upper_block % blocks_here,
        0,
        column_count - 1,
    )
    roster_step_count = (roster_pair_count + tiles_per_step - 1) // tiles_per_step
    plan = (
        roster_first_pair,
        roster_pair_count,
        roster_row_slot,
        roster_column_slot,
        roster_step_count,
        lower_block.shape[0],
    )
    first_pair, pair_count, row_slot, column_slot, step_count, listed = plan
    own_tiles = covariance_tiles(own_blocks, own_blocks).astype(jnp.bfloat16)

    def pick_tiles(step):
        offsets = step * tiles_per_step + jnp.arange(tiles_per_step)
        usable = offsets < pair_count
        picked = jnp.minimum(first_pair + offsets, listed - 1)
        row_pick = row_slot[picked]
        column_pick = column_slot[picked]
        tiles_now = covariance_tiles(row_blocks[row_pick], column_blocks[column_pick])
        tiles_now = jnp.where(usable[:, None, None], tiles_now, 0.0).astype(jnp.bfloat16)
        return (tiles_now, row_pick, column_pick)

    def inner(operands):
        stacked = jnp.stack(
            [jnp.sum(one_side * other_side, axis=1) for one_side, other_side in operands]
        )
        return lax.psum(stacked, ("row", "col"))

    solution = jnp.zeros_like(right_side)
    residual = right_side
    direction = right_side
    norm_now = inner(((residual, residual),))[0]
    for step in range(ITERS):
        rounded = direction.astype(jnp.bfloat16)
        product_row_direction = lax.all_gather(rounded, "col", axis=1, tiled=True)
        product_column_direction = lax.all_gather(rounded, "row", axis=1, tiled=True)
        row_direction = product_row_direction
        column_direction = product_column_direction
        row_direction = row_direction.reshape(realizations, row_count, BLOCK)
        column_direction = column_direction.reshape(realizations, column_count, BLOCK)

        def add_step(step, totals):
            into_rows, into_columns = totals
            tiles_now, row_pick, column_pick = pick_tiles(step)
            to_rows = jnp.einsum(
                "tij,ctj->cti",
                tiles_now,
                column_direction[:, column_pick],
                preferred_element_type=jnp.float32,
            )
            to_columns = jnp.einsum(
                "tij,cti->ctj",
                tiles_now,
                row_direction[:, row_pick],
                preferred_element_type=jnp.float32,
            )
            return (
                into_rows.at[:, row_pick].add(to_rows),
                into_columns.at[:, column_pick].add(to_columns),
            )

        empty_rows = jnp.zeros((realizations, row_count, BLOCK), jnp.float32)
        empty_columns = jnp.zeros((realizations, column_count, BLOCK), jnp.float32)
        into_rows, into_columns = lax.fori_loop(
            0, step_count, add_step, (empty_rows, empty_columns)
        )
        product_into_rows = into_rows.reshape(realizations, -1)
        product_into_columns = into_columns.reshape(realizations, -1)
        from_rows = lax.psum_scatter(product_into_rows, "col", scatter_dimension=1, tiled=True)
        from_columns = lax.psum_scatter(
            product_into_columns.astype(jnp.bfloat16), "row", scatter_dimension=1, tiled=True
        ).astype(jnp.float32)
        diagonal = jnp.einsum(
            "tij,ctj->cti",
            own_tiles,
            rounded.reshape(realizations, blocks_here, BLOCK),
            preferred_element_type=jnp.float32,
        )
        image = (
            nugget * direction + diagonal.reshape(realizations, points) + from_rows + from_columns
        )
        alpha = norm_now / inner(((direction, image),))[0]
        solution = solution + alpha[:, None] * direction
        residual = residual - alpha[:, None] * image
        if step + 1 < ITERS:
            norm_next = inner(((residual, residual),))[0]
            direction = residual + (norm_next / norm_now)[:, None] * direction
            norm_now = norm_next
    return (solution, residual)


def tile_schedule(listed, blocks):
    half = (listed + 1) // 2
    entries = half + blocks // 2
    sizes = range(12, 25)
    width = min(sizes, key=lambda size: (-(-entries // size) * size, -size))
    steps = -(-entries // width)
    longest = (2 * half + blocks // 2 + 3 * blocks) // chunk
    chunks = -(-longest // chunks_per_step) * chunks_per_step + chunks_per_step
    return half, width, steps, chunks


def radial(squared):
    squared = jnp.maximum(squared, 1e-30)
    distance = squared * lax.rsqrt(squared)
    near = jnp.maximum(long_range - distance, 0.0)
    close = jnp.maximum(short_range - distance, 0.0)

    def falling(remain, reach):
        square = remain * remain
        return square * square * (5.0 / reach**4 - 4.0 / reach**5 * remain)

    return (falling(near, long_range) + falling(close, short_range)).astype(bf16)


def three_parts(values):
    first = values.astype(bf16).astype(f32)
    rest = values - first
    second = rest.astype(bf16).astype(f32)
    return first, second, rest - second


def row_number(shape):
    return lax.broadcasted_iota(jnp.int32, shape, len(shape) - 2)


def store_scaled(fields_ref, direction, scale):
    scaled = jnp.where(row_number(direction.shape) < rows_here, direction * scale, 0.0)
    blocks = direction.shape[0]
    doubled = jnp.concatenate([scaled, jnp.zeros_like(scaled)], axis=1)
    fields_ref[0:blocks] = doubled.astype(bf16)
    fields_ref[blocks] = jnp.zeros((16, BLOCK), bf16)


def multiply(owner_ref, entry_ref, count, tiles_ref, fields_ref, totals_ref):
    totals_ref[...] = jnp.zeros_like(totals_ref)

    def step(number, carry):
        products = []
        for part in range(chunks_per_step):
            fields = []
            tiles = []
            for slot in range(chunk):
                entry = entry_ref[(number * chunks_per_step + part) * chunk + slot]
                fields.append(fields_ref[entry & 65535])
                tiles.append(tiles_ref[entry >> 16])
            product = jnp.dot(
                jnp.concatenate(fields, axis=1),
                jnp.concatenate(tiles, axis=0),
                preferred_element_type=f32,
            )
            products.append(product[0:8])
        for part in range(chunks_per_step):
            totals_ref[owner_ref[number * chunks_per_step + part]] += products[part]
        return carry

    lax.fori_loop(0, (count + chunks_per_step - 1) // chunks_per_step, step, 0)


def first_kernel(
    plan,
    core_ref,
    pair_ref,
    gathered_ref,
    tiles_ref,
    product_ref,
    owner_ref,
    entry_ref,
    count_ref,
    left_ref,
    right_ref,
    fields_ref,
    totals_ref,
    length_ref,
    open_ref,
):
    half, width, steps, chunks = plan
    blocks = gathered_ref.shape[0]
    listed = pair_ref.shape[1]
    core = core_ref[0]
    slots = width * steps
    highest = jnp.max(jnp.max(gathered_ref[...], axis=0), axis=1, keepdims=True)
    lowest = jnp.min(jnp.min(gathered_ref[...], axis=0), axis=1, keepdims=True)
    centre = 0.5 * (highest + lowest)

    def prepare(block, carry):
        row = row_number((8, BLOCK))
        is_coordinate = (row >= 4) & (row < 7)
        shifted = jnp.where(is_coordinate, gathered_ref[block] - centre, 0.0)
        squared = jnp.sum(shifted * shifted, axis=0, keepdims=True)
        left = jnp.where(row == 7, 1.0, jnp.where(row == 0, squared, shifted))
        right = jnp.where(row == 7, squared, jnp.where(row == 0, 1.0, -2.0 * shifted))
        left_1, left_2, left_3 = three_parts(left)
        right_1, right_2, right_3 = three_parts(right)
        left_all = jnp.concatenate([left_1, left_1, left_2, left_2, left_1, left_3], axis=0)
        right_all = jnp.concatenate([right_1, right_2, right_1, right_2, right_3, right_1], axis=0)
        left_ref[block] = left_all.T.astype(bf16)
        right_ref[block] = right_all.astype(bf16)
        length_ref[block] = 0
        return carry

    lax.fori_loop(0, blocks, prepare, 0, unroll=4)
    length_ref[blocks] = 0
    open_ref[blocks] = 0
    spare = chunks * chunk
    empty = blocks

    def append(block, entry, usable, used):
        length = length_ref[block]
        place = length & (chunk - 1)
        fresh = place == 0
        where = jnp.where(fresh, used, open_ref[block])
        begins = fresh & usable
        target = jnp.where(usable, block, blocks)
        length_ref[target] = length + 1
        open_ref[target] = where
        for slot in range(1, chunk):
            entry_ref[jnp.where(begins, where * chunk + slot, spare)] = empty
        entry_ref[jnp.where(usable, where * chunk + place, spare)] = entry
        owner_ref[jnp.where(usable, where, chunks)] = block
        return used + begins.astype(jnp.int32)

    def make_tiles(step, used):
        for slot in range(width):
            number = step * width + slot
            is_pair = number < half
            pair = core * half + number
            is_diagonal = (number >= half) & (number < half + blocks // 2)
            pair_usable = is_pair & (pair < listed)
            safe = jnp.minimum(pair, listed - 1)
            own = jnp.minimum(core * (blocks // 2) + number - half, blocks - 1)
            low = jnp.where(is_pair, pair_ref[0, safe], own)
            high = jnp.where(is_pair, pair_ref[1, safe], own)
            squared = jnp.dot(left_ref[low], right_ref[high], preferred_element_type=f32)
            tile = radial(squared)
            tiles_ref[number] = tile
            tiles_ref[slots + number] = tile.T
            used = append(high, number * 65536 + low, pair_usable | is_diagonal, used)
            used = append(low, (slots + number) * 65536 + high, pair_usable, used)
        return used

    used = lax.fori_loop(0, steps, make_tiles, 0)
    count_ref[0] = used
    for part in range(chunks_per_step):
        owner_ref[used + part] = blocks
        for slot in range(chunk):
            entry_ref[(used + part) * chunk + slot] = empty
    store_scaled(fields_ref, gathered_ref[...], gathered_ref[:, 7:8, :])
    multiply(owner_ref, entry_ref, used, tiles_ref, fields_ref, totals_ref)
    product_ref[...] = totals_ref[0:blocks]


def total(values):
    return jnp.sum(jnp.sum(values, axis=0), axis=1, keepdims=True)[None]


def advance(mine_ref, other_ref, scale, direction, residual):
    row = row_number((1, 8, 1))
    image = nugget * direction + scale * (mine_ref[...] + other_ref[...])
    norm_now = total(residual * residual)
    along = total(direction * image)
    alpha = norm_now / jnp.where(row < rows_here, along, 1.0)
    return alpha * direction, residual - alpha * image, norm_now


def next_kernel(
    first,
    owner_ref,
    entry_ref,
    count_ref,
    gathered_ref,
    mine_ref,
    other_ref,
    *rest,
):
    if first:
        tiles_ref, product_ref, state_out_ref, fields_ref, totals_ref = rest
        row = row_number(gathered_ref.shape)
        direction = jnp.where(row < rows_here, gathered_ref[...], 0.0)
        residual = direction
    else:
        state_ref, tiles_ref, product_ref, state_out_ref, fields_ref, totals_ref = rest
        direction = state_ref[2]
        residual = state_ref[1]
    scale = gathered_ref[:, 7:8, :]
    moved, residual, norm_now = advance(mine_ref, other_ref, scale, direction, residual)
    norm_next = total(residual * residual)
    row = row_number((1, 8, 1))
    beta = norm_next / jnp.where(row < rows_here, norm_now, 1.0)
    direction = residual + beta * direction
    state_out_ref[0] = moved if first else state_ref[0] + moved
    state_out_ref[1] = residual
    state_out_ref[2] = direction
    store_scaled(fields_ref, direction, scale)
    multiply(owner_ref, entry_ref, count_ref[0], tiles_ref, fields_ref, totals_ref)
    product_ref[...] = totals_ref[0 : gathered_ref.shape[0]]


def last_kernel(core_ref, gathered_ref, mine_ref, other_ref, state_ref, result_ref):
    scale = gathered_ref[:, 7:8, :]
    moved, residual, _ = advance(mine_ref, other_ref, scale, state_ref[2], state_ref[1])
    chosen = jnp.where(core_ref[0] == 0, state_ref[0] + moved, residual)
    result_ref[...] = chosen[:, 0:rows_here, :]


def by_realizations(point_data, right_side, pair_list):
    col_devices = lax.axis_size("col")
    devices = lax.axis_size("row") * col_devices
    chips = devices // 2
    blocks_here = point_data.shape[1] // BLOCK
    blocks = blocks_here * devices
    core = lax.rem(lax.axis_index("col"), 2).astype(jnp.int32).reshape(1)
    axes = ("row", "col")
    vector = pl.BlockSpec(memory_space=pltpu.VMEM)
    scalar = pl.BlockSpec(memory_space=pltpu.SMEM)
    plan = tile_schedule(pair_list.shape[1], blocks)
    half, width, steps, chunks = plan
    slots = width * steps

    points = point_data.reshape(1, 4, blocks_here, BLOCK).transpose(0, 2, 1, 3)
    fields = right_side.reshape(chips, rows_here, blocks_here, BLOCK).transpose(0, 2, 1, 3)
    points = jnp.broadcast_to(points, (chips, blocks_here, 4, BLOCK))
    outgoing = jnp.concatenate([fields, points], axis=2)
    outgoing = jnp.broadcast_to(outgoing[:, None], (chips, 2, blocks_here, 8, BLOCK))
    outgoing = outgoing.reshape(devices, blocks_here, 8, BLOCK)
    gathered = lax.all_to_all(outgoing, axes, 0, 0, tiled=True).reshape(blocks, 8, BLOCK)

    field_shape = jax.ShapeDtypeStruct((blocks, 8, BLOCK), f32)
    state_shape = jax.ShapeDtypeStruct((3, blocks, 8, BLOCK), f32)
    work = [pltpu.VMEM((blocks + 1, 16, BLOCK), bf16), pltpu.VMEM((blocks + 1, 8, BLOCK), f32)]
    limits = pltpu.CompilerParams(vmem_limit_bytes=kernel_bytes)
    tiles, mine, owner, entry, count = pl.pallas_call(
        functools.partial(first_kernel, plan),
        out_shape=(
            pltpu.VMEM((2 * slots, BLOCK, BLOCK), bf16),
            field_shape,
            jax.ShapeDtypeStruct((chunks + 8,), jnp.int32),
            jax.ShapeDtypeStruct((chunks * chunk + 8,), jnp.int32),
            jax.ShapeDtypeStruct((1,), jnp.int32),
        ),
        in_specs=[scalar, scalar, vector],
        out_specs=(vector, vector, scalar, scalar, scalar),
        scratch_shapes=[
            pltpu.VMEM((blocks, BLOCK, 48), bf16),
            pltpu.VMEM((blocks, 48, BLOCK), bf16),
            *work,
            pltpu.SMEM((blocks + 8,), jnp.int32),
            pltpu.SMEM((blocks + 8,), jnp.int32),
        ],
        compiler_params=limits,
    )(core, pair_list, gathered)
    tiles = pltpu.with_memory_space_constraint(tiles, pltpu.VMEM)
    swap = [(place, place ^ 1) for place in range(col_devices)]
    state = None
    for step in range(1, ITERS):
        other = lax.ppermute(mine, "col", swap)
        first = step == 1
        carried = () if first else (state,)
        mine, state = pl.pallas_call(
            functools.partial(next_kernel, first),
            out_shape=(field_shape, state_shape),
            in_specs=[scalar, scalar, scalar] + [vector] * (4 + len(carried)),
            out_specs=(vector, vector),
            scratch_shapes=work,
            compiler_params=limits,
        )(owner, entry, count, gathered, mine, other, *carried, tiles)
    other = lax.ppermute(mine, "col", swap)
    result = pl.pallas_call(
        last_kernel,
        out_shape=jax.ShapeDtypeStruct((blocks, rows_here, BLOCK), f32),
        in_specs=[scalar] + [vector] * 4,
        out_specs=vector,
        compiler_params=limits,
    )(core, gathered, mine, other, state)
    result = result.reshape(devices, blocks_here, rows_here, BLOCK)
    received = lax.all_to_all(result, axes, 0, 0, tiled=True)
    received = received.reshape(chips, 2, blocks_here, rows_here, BLOCK)
    received = received.transpose(1, 0, 3, 2, 4).reshape(2, right_side.shape[0], -1)
    return received[0], received[1]


def per_device(point_data, right_side, pair_list):
    col_devices = lax.axis_size("col")
    devices = lax.axis_size("row") * col_devices
    blocks = point_data.shape[1] // BLOCK * devices
    _, width, steps, _ = tile_schedule(pair_list.shape[1], blocks)
    tile_bytes = 2 * width * steps * BLOCK * BLOCK * 2
    paired = col_devices % 2 == 0 and blocks % 2 == 0
    if paired and right_side.shape[0] == rows_here * (devices // 2) and tile_bytes <= tile_bytes_limit:
        return by_realizations(point_data, right_side, pair_list)
    return by_points(point_data, right_side, pair_list)


def solution(mesh):
    placed = (P(None, ("row", "col")), P(None, ("row", "col")), P())
    return jax.shard_map(
        per_device,
        mesh=mesh,
        in_specs=placed,
        out_specs=(P(None, ("row", "col")), P(None, ("row", "col"))),
        check_vma=False,
    )
```

profile of v0, /device:TPU:0, one launch (start us, length us, event | category | flops | bytes accessed | tf_op | source)
XLA Modules:
  0.0 77.2 jit_solution(1675590507653392535)
XLA Ops:
  0.6 0.7 reshape.33
  1.3 0.9 %reshape.32 = f32[16,4,2,128]{3,2,1,0:T(2,128)S(1)} reshape(f32[64,256]{1,0:T(8,128)} %param.4) | data formatting | bytes 131072 | tf_op jit(solution)/shard_map/reshape | solution.py:393
  2.2 0.1 pad_maximum_fusion
  2.3 0.7 broadcast_in_dim.15
  3.1 7.3 %all-to-all-start = ((f32[32,2,8,128]{3,2,1,0:T(8,128)}), f32[32,2,8,128]{3,2,1,0:T(8,128)S(1)}, u32[]{:S(2)}, u32[]{:S(2)}) async-start(f32[32,2,8,128]{3,2,1,0:T(8,128)} %bitcast.4), calls=%async_computation | async-start | bytes 524288 | tf_op jit(solution)/shard_map/all_to_all | solution.py:398
  10.4 10.6 %all-to-all-done = f32[32,2,8,128]{3,2,1,0:T(8,128)S(1)} async-done(((f32[32,2,8,128]{3,2,1,0:T(8,128)}), f32[32,2,8,128]{3,2,1,0:T(8,128)S(1)}, u32[]{:S(2)}, u32[]{:S(2)}) %all-to-all-start) | async-done | bytes 262176 | tf_op jit(solution)/shard_map/all_to_all | solution.py:398
  21.0 0.0 copy-start
  21.0 0.7 copy-done
  21.6 26.6 %shard_map.50 = (bf16[532,128,128]{2,1,0:T(8,128)(2,1)S(1)}, f32[64,8,128]{2,1,0:T(8,128)S(1)}, s32[192]{0:T(256)S(1)}, s32[744]{0:T(1024)S(1)}, s32[1]{0:T(128)}) custom-call(s32[1]{0:T(128)} %bitcast.core_ref, s32[2,468]{1,0:T(2,128)S(1)} %copy-done, f32[64,8,128]{2,1,0:T(8,128)S(1)} %bitcast.20), custom_call_target="tpu_custom_call" | custom-call | tf_op jit(solution)/shard_map/pallas_call | solution.py:404
  48.2 0.1 collective-permute-start
  48.3 1.5 %collective-permute-done.other_ref = f32[64,8,128]{2,1,0:T(8,128)S(1)} collective-permute-done((f32[64,8,128]{2,1,0:T(8,128)S(1)}, f32[64,8,128]{2,1,0:T(8,128)S(1)}, u32[]{:S(2)}, u32[]{:S(2)}) %collective-permute-start) | collective-permute-done | bytes 262176 | tf_op jit(solution)/shard_map/ppermute | solution.py:428
  49.8 6.3 %shard_map.51 = (f32[64,8,128]{2,1,0:T(8,128)S(1)}, f32[3,64,8,128]{3,2,1,0:T(8,128)S(1)}) custom-call(s32[192]{0:T(256)S(1)} %get-tuple-element.11.owner_ref, s32[744]{0:T(1024)S(1)} %get-tuple-element.12.entry_ref, s32[1]{0:T(128)} %get-tuple-element.13.count_ref, f32[64,8,128]{2,1,0:T(8,128)S(1)} %bitcast.21, ...), custom_call_target="tpu_custom_call" | custom-call | tf_op jit(solution)/shard_map/pallas_call | solution.py:431
  56.2 0.2 collective-permute-start.1
  56.4 1.4 %collective-permute-done.1.other_ref = f32[64,8,128]{2,1,0:T(8,128)S(1)} collective-permute-done((f32[64,8,128]{2,1,0:T(8,128)S(1)}, f32[64,8,128]{2,1,0:T(8,128)S(1)}, u32[]{:S(2)}, u32[]{:S(2)}) %collective-permute-start.1) | collective-permute-done | bytes 262176 | tf_op jit(solution)/shard_map/ppermute | solution.py:428
  57.8 6.3 %shard_map.52 = (f32[64,8,128]{2,1,0:T(8,128)S(1)}, f32[3,64,8,128]{3,2,1,0:T(8,128)S(1)}) custom-call(s32[192]{0:T(256)S(1)} %get-tuple-element.11.owner_ref, s32[744]{0:T(1024)S(1)} %get-tuple-element.12.entry_ref, s32[1]{0:T(128)} %get-tuple-element.13.count_ref, f32[64,8,128]{2,1,0:T(8,128)S(1)} %bitcast.22, ...), custom_call_target="tpu_custom_call" | custom-call | tf_op jit(solution)/shard_map/pallas_call | solution.py:431
  64.1 0.2 collective-permute-start.2
  64.3 1.4 %collective-permute-done.2.other_ref = f32[64,8,128]{2,1,0:T(8,128)S(1)} collective-permute-done((f32[64,8,128]{2,1,0:T(8,128)S(1)}, f32[64,8,128]{2,1,0:T(8,128)S(1)}, u32[]{:S(2)}, u32[]{:S(2)}) %collective-permute-start.2) | collective-permute-done | bytes 262176 | tf_op jit(solution)/shard_map/ppermute | solution.py:439
  65.7 0.3 shard_map.53
  66.0 10.4 %all_to_all.10 = f32[32,2,4,128]{3,2,1,0:T(4,128)S(1)} all-to-all(f32[32,2,4,128]{3,2,1,0:T(4,128)S(1)} %bitcast.24), channel_id=1, replica_groups=mesh['row'=4,'col'=8] {'row','col'}, dimensions={0} | all-to-all | bytes 262144 | tf_op jit(solution)/shard_map/all_to_all | solution.py:448
  76.4 0.1 copy.12
  76.5 0.7 copy_bitcast_fusion.1
  (3 shorter events, 0.0 us)
Async XLA Ops:
  3.1 17.9 %all-to-all-start = ((f32[32,2,8,128]{3,2,1,0:T(8,128)}), f32[32,2,8,128]{3,2,1,0:T(8,128)S(1)}, u32[]{:S(2)}, u32[]{:S(2)}) async-start(f32[32,2,8,128]{3,2,1,0:T(8,128)} %bitcast.4), calls=%async_computation | async-start | bytes 524288 | tf_op jit(solution)/shard_map/all_to_all | solution.py:398
  21.0 0.7 copy-start
  48.2 1.6 %collective-permute-start = (f32[64,8,128]{2,1,0:T(8,128)S(1)}, f32[64,8,128]{2,1,0:T(8,128)S(1)}, u32[]{:S(2)}, u32[]{:S(2)}) collective-permute-start(f32[64,8,128]{2,1,0:T(8,128)S(1)} %get-tuple-element.14.mine_ref), channel_id=1, source_target_pairs={{0,1},{1,0},{2,3},{3,2},{4,5},{5,4},{6,7},{7,6},{8,9},{9,8},{10,11... | collective-permute-start | bytes 786440 | tf_op jit(solution)/shard_map/ppermute | solution.py:428
  56.2 1.6 %collective-permute-start.1 = (f32[64,8,128]{2,1,0:T(8,128)S(1)}, f32[64,8,128]{2,1,0:T(8,128)S(1)}, u32[]{:S(2)}, u32[]{:S(2)}) collective-permute-start(f32[64,8,128]{2,1,0:T(8,128)S(1)} %get-tuple-element.16.mine_ref), channel_id=1, source_target_pairs={{0,1},{1,0},{2,3},{3,2},{4,5},{5,4},{6,7},{7,6},{8,9},{9,8},{10,11... | collective-permute-start | bytes 786440 | tf_op jit(solution)/shard_map/ppermute | solution.py:428
  64.1 1.6 %collective-permute-start.2 = (f32[64,8,128]{2,1,0:T(8,128)S(1)}, f32[64,8,128]{2,1,0:T(8,128)S(1)}, u32[]{:S(2)}, u32[]{:S(2)}) collective-permute-start(f32[64,8,128]{2,1,0:T(8,128)S(1)} %get-tuple-element.18.mine_ref), channel_id=1, source_target_pairs={{0,1},{1,0},{2,3},{3,2},{4,5},{5,4},{6,7},{7,6},{8,9},{9,8},{10,11... | collective-permute-start | bytes 786440 | tf_op jit(solution)/shard_map/ppermute | solution.py:439
where the time goes:
time: 77.9 us; the launch traced here: 77.2 us
  Pallas kernels  39.5 us (51%)
  waiting for transfers between devices  14.9 us (19%)
  blocking collectives  10.4 us (13%)
  starting transfers between devices  7.77 us (10%)
  local copies, waits for them, and re-layouts  3.76 us (5%)
    pallas_call x1, Pallas kernels, by_realizations(): pl.pallas_call(functools.partial(first_kernel, plan), out_shape=(pltpu.VM...  26.6 us
    pallas_call x2, Pallas kernels, by_realizations(): pl.pallas_call(functools.partial(next_kernel, first), out_shape=(field_sh...  12.7 us
    all_to_all x1, waiting for transfers between devices, by_realizations(): lax.all_to_all(outgoing, axes, 0, 0, tiled=True).reshape(blocks, 8, BLOCK)  10.6 us
    all_to_all x1, blocking collectives, by_realizations(): received = lax.all_to_all(result, axes, 0, 0, tiled=True)  10.4 us
    all_to_all x1, starting transfers between devices, by_realizations(): lax.all_to_all(outgoing, axes, 0, 0, tiled=True).reshape(blocks, 8, BLOCK)  7.3 us
    ppermute x3, waiting for transfers between devices, by_realizations(): other = lax.ppermute(mine, 'col', swap)  4.32 us
  transfers between devices with their start and end apart: 4, of which 4 were waited for; matrix products, arithmetic and copies ran while one was open for 0% of the time, Pallas kernels for 0%

commit v1 on v0

--- a/solution.py
+++ b/solution.py
@@ -164,12 +164,92 @@
 def tile_schedule(listed, blocks):
     half = (listed + 1) // 2
     entries = half + blocks // 2
-    sizes = range(12, 25)
-    width = min(sizes, key=lambda size: (-(-entries // size) * size, -size))
-    steps = -(-entries // width)
+    sizes = range(12, 21)
+    width = min(sizes, key=lambda size: (-(-entries // (2 * size)) * size, -size))
+    steps = -(-entries // (2 * width)) * 2
     longest = (2 * half + blocks // 2 + 3 * blocks) // chunk
     chunks = -(-longest // chunks_per_step) * chunks_per_step + chunks_per_step
     return half, width, steps, chunks
+
+
+def packing_kernel(point_hbm, field_hbm, outgoing_ref, point_ref, field_ref, arrived):
+    devices, blocks_here = outgoing_ref.shape[0:2]
+    copies = (
+        pltpu.make_async_copy(point_hbm, point_ref, arrived.at[0]),
+        pltpu.make_async_copy(field_hbm, field_ref, arrived.at[1]),
+    )
+    for copy in copies:
+        copy.start()
+    for copy in copies:
+        copy.wait()
+    for chip in range(devices // 2):
+        for block in range(blocks_here):
+            place = pl.ds(block * BLOCK, BLOCK)
+            fields = field_ref[pl.ds(chip * rows_here, rows_here), place]
+            both = jnp.concatenate([fields, point_ref[:, place]], axis=0)
+            outgoing_ref[2 * chip, block] = both
+            outgoing_ref[2 * chip + 1, block] = both
+
+
+def entry_blocks(plan, blocks, core, pair_ref, number):
+    half = plan[0]
+    listed = pair_ref.shape[1]
+    pair = core * half + number
+    is_pair = number < half
+    pair_usable = is_pair & (pair < listed)
+    usable = pair_usable | ((number >= half) & (number < half + blocks // 2))
+    safe = jnp.minimum(pair, listed - 1)
+    own = jnp.minimum(core * (blocks // 2) + number - half, blocks - 1)
+    low = jnp.where(is_pair, pair_ref[0, safe], own)
+    high = jnp.where(is_pair, pair_ref[1, safe], own)
+    return low, high, usable, pair_usable
+
+
+def listing_kernel(
+    plan, blocks, core_ref, pair_ref, owner_ref, entry_ref, count_ref, length_ref, open_ref
+):
+    _, width, steps, chunks = plan
+    core = core_ref[0]
+    slots = width * steps
+    spare = chunks * chunk
+    empty = blocks
+
+    def clear(block, carry):
+        length_ref[block] = 0
+        open_ref[block] = 0
+        return carry
+
+    lax.fori_loop(0, blocks + 1, clear, 0)
+
+    def append(block, entry, usable, used):
+        length = length_ref[block]
+        place = length & (chunk - 1)
+        fresh = place == 0
+        where = jnp.where(fresh, used, open_ref[block])
+        begins = fresh & usable
+        target = jnp.where(usable, block, blocks)
+        length_ref[target] = length + 1
+        open_ref[target] = where
+        for slot in range(1, chunk):
+            entry_ref[jnp.where(begins, where * chunk + slot, spare)] = empty
+        entry_ref[jnp.where(usable, where * chunk + place, spare)] = entry
+        owner_ref[jnp.where(usable, where, chunks)] = block
+        return used + begins.astype(jnp.int32)
+
+    def list_tiles(step, used):
+        for slot in range(width):
+            number = step * width + slot
+            low, high, usable, pair_usable = entry_blocks(plan, blocks, core, pair_ref, number)
+            used = append(high, number * 65536 + low, usable, used)
+            used = append(low, (slots + number) * 65536 + high, pair_usable, used)
+        return used
+
+    used = lax.fori_loop(0, steps, list_tiles, 0)
+    count_ref[0] = used
+    for part in range(chunks_per_step):
+        owner_ref[used + part] = blocks
+        for slot in range(chunk):
+            entry_ref[(used + part) * chunk + slot] = empty
 
 
 def radial(squared):
@@ -232,23 +312,19 @@
 def first_kernel(
     plan,
     core_ref,
+    count_ref,
     pair_ref,
     gathered_ref,
     tiles_ref,
     product_ref,
-    owner_ref,
-    entry_ref,
-    count_ref,
     left_ref,
     right_ref,
     fields_ref,
     totals_ref,
-    length_ref,
-    open_ref,
+    *stages,
 ):
-    half, width, steps, chunks = plan
+    _, width, steps, _ = plan
     blocks = gathered_ref.shape[0]
-    listed = pair_ref.shape[1]
     core = core_ref[0]
     slots = width * steps
     highest = jnp.max(jnp.max(gathered_ref[...], axis=0), axis=1, keepdims=True)
@@ -268,57 +344,52 @@
         right_all = jnp.concatenate([right_1, right_2, right_1, right_2, right_3, right_1], axis=0)
         left_ref[block] = left_all.T.astype(bf16)
         right_ref[block] = right_all.astype(bf16)
-        length_ref[block] = 0
         return carry
 
-    lax.fori_loop(0, blocks, prepare, 0, unroll=4)
-    length_ref[blocks] = 0
-    open_ref[blocks] = 0
-    spare = chunks * chunk
-    empty = blocks
-
-    def append(block, entry, usable, used):
-        length = length_ref[block]
-        place = length & (chunk - 1)
-        fresh = place == 0
-        where = jnp.where(fresh, used, open_ref[block])
-        begins = fresh & usable
-        target = jnp.where(usable, block, blocks)
-        length_ref[target] = length + 1
-        open_ref[target] = where
-        for slot in range(1, chunk):
-            entry_ref[jnp.where(begins, where * chunk + slot, spare)] = empty
-        entry_ref[jnp.where(usable, where * chunk + place, spare)] = entry
-        owner_ref[jnp.where(usable, where, chunks)] = block
-        return used + begins.astype(jnp.int32)
-
-    def make_tiles(step, used):
+    lax.fori_loop(0, blocks, prepare, 0, unroll=8)
+    store_scaled(fields_ref, gathered_ref[...], gathered_ref[:, 7:8, :])
+    totals_ref[...] = jnp.zeros_like(totals_ref)
+
+    def make_tiles(step, stage):
         for slot in range(width):
             number = step * width + slot
-            is_pair = number < half
-            pair = core * half + number
-            is_diagonal = (number >= half) & (number < half + blocks // 2)
-            pair_usable = is_pair & (pair < listed)
-            safe = jnp.minimum(pair, listed - 1)
-            own = jnp.minimum(core * (blocks // 2) + number - half, blocks - 1)
-            low = jnp.where(is_pair, pair_ref[0, safe], own)
-            high = jnp.where(is_pair, pair_ref[1, safe], own)
+            low, high, _, _ = entry_blocks(plan, blocks, core, pair_ref, number)
             squared = jnp.dot(left_ref[low], right_ref[high], preferred_element_type=f32)
             tile = radial(squared)
+            turned = tile.T
             tiles_ref[number] = tile
-            tiles_ref[slots + number] = tile.T
-            used = append(high, number * 65536 + low, pair_usable | is_diagonal, used)
-            used = append(low, (slots + number) * 65536 + high, pair_usable, used)
-        return used
-
-    used = lax.fori_loop(0, steps, make_tiles, 0)
-    count_ref[0] = used
-    for part in range(chunks_per_step):
-        owner_ref[used + part] = blocks
-        for slot in range(chunk):
-            entry_ref[(used + part) * chunk + slot] = empty
-    store_scaled(fields_ref, gathered_ref[...], gathered_ref[:, 7:8, :])
-    multiply(owner_ref, entry_ref, used, tiles_ref, fields_ref, totals_ref)
+            tiles_ref[slots + number] = turned
+            stage[0][slot] = tile
+            stage[1][slot] = turned
+
+    def use_tiles(step, stage):
+        products = []
+        for slot in range(width):
+            number = step * width + slot
+            low, high, usable, pair_usable = entry_blocks(plan, blocks, core, pair_ref, number)
+            usable = usable & (number >= 0)
+            pair_usable = pair_usable & (number >= 0)
+            ways = (
+                (jnp.where(usable, low, blocks), jnp.where(usable, high, blocks)),
+                (jnp.where(pair_usable, high, blocks), jnp.where(pair_usable, low, blocks)),
+            )
+            for (source, target), tiles in zip(ways, stage):
+                product = jnp.dot(fields_ref[source], tiles[slot], preferred_element_type=f32)
+                products.append((target, product[0:8]))
+        for target, product in products:
+            totals_ref[target] += product
+
+    even, odd = stages[0:2], stages[2:4]
+
+    def both_steps(pair, carry):
+        make_tiles(2 * pair, even)
+        use_tiles(2 * pair - 1, odd)
+        make_tiles(2 * pair + 1, odd)
+        use_tiles(2 * pair, even)
+        return carry
+
+    lax.fori_loop(0, steps // 2, both_steps, 0)
+    use_tiles(steps - 1, odd)
     product_ref[...] = totals_ref[0:blocks]
 
 
@@ -389,38 +460,54 @@
     half, width, steps, chunks = plan
     slots = width * steps
 
-    points = point_data.reshape(1, 4, blocks_here, BLOCK).transpose(0, 2, 1, 3)
-    fields = right_side.reshape(chips, rows_here, blocks_here, BLOCK).transpose(0, 2, 1, 3)
-    points = jnp.broadcast_to(points, (chips, blocks_here, 4, BLOCK))
-    outgoing = jnp.concatenate([fields, points], axis=2)
-    outgoing = jnp.broadcast_to(outgoing[:, None], (chips, 2, blocks_here, 8, BLOCK))
-    outgoing = outgoing.reshape(devices, blocks_here, 8, BLOCK)
-    gathered = lax.all_to_all(outgoing, axes, 0, 0, tiled=True).reshape(blocks, 8, BLOCK)
-
-    field_shape = jax.ShapeDtypeStruct((blocks, 8, BLOCK), f32)
-    state_shape = jax.ShapeDtypeStruct((3, blocks, 8, BLOCK), f32)
-    work = [pltpu.VMEM((blocks + 1, 16, BLOCK), bf16), pltpu.VMEM((blocks + 1, 8, BLOCK), f32)]
     limits = pltpu.CompilerParams(vmem_limit_bytes=kernel_bytes)
-    tiles, mine, owner, entry, count = pl.pallas_call(
-        functools.partial(first_kernel, plan),
+    outgoing = pl.pallas_call(
+        packing_kernel,
+        out_shape=jax.ShapeDtypeStruct((devices, blocks_here, 8, BLOCK), f32),
+        in_specs=[pl.BlockSpec(memory_space=pltpu.HBM)] * 2,
+        out_specs=vector,
+        scratch_shapes=[
+            pltpu.VMEM(point_data.shape, f32),
+            pltpu.VMEM(right_side.shape, f32),
+            pltpu.SemaphoreType.DMA((2,)),
+        ],
+        compiler_params=limits,
+    )(
+        pltpu.with_memory_space_constraint(point_data, pltpu.HBM),
+        pltpu.with_memory_space_constraint(right_side, pltpu.HBM),
+    )
+    owner, entry, count = pl.pallas_call(
+        functools.partial(listing_kernel, plan, blocks),
         out_shape=(
-            pltpu.VMEM((2 * slots, BLOCK, BLOCK), bf16),
-            field_shape,
             jax.ShapeDtypeStruct((chunks + 8,), jnp.int32),
             jax.ShapeDtypeStruct((chunks * chunk + 8,), jnp.int32),
             jax.ShapeDtypeStruct((1,), jnp.int32),
         ),
-        in_specs=[scalar, scalar, vector],
-        out_specs=(vector, vector, scalar, scalar, scalar),
+        in_specs=[scalar, scalar],
+        out_specs=(scalar, scalar, scalar),
+        scratch_shapes=[pltpu.SMEM((blocks + 8,), jnp.int32)] * 2,
+        cost_estimate=pl.CostEstimate(flops=8_000_000_000, bytes_accessed=20_000_000, transcendentals=0),
+        compiler_params=limits,
+    )(core, pair_list)
+    gathered = lax.all_to_all(outgoing, axes, 0, 0, tiled=True).reshape(blocks, 8, BLOCK)
+
+    field_shape = jax.ShapeDtypeStruct((blocks, 8, BLOCK), f32)
+    state_shape = jax.ShapeDtypeStruct((3, blocks, 8, BLOCK), f32)
+    work = [pltpu.VMEM((blocks + 1, 16, BLOCK), bf16), pltpu.VMEM((blocks + 1, 8, BLOCK), f32)]
+    stage = pltpu.VMEM((width, BLOCK, BLOCK), bf16)
+    tiles, mine = pl.pallas_call(
+        functools.partial(first_kernel, plan),
+        out_shape=(pltpu.VMEM((2 * slots, BLOCK, BLOCK), bf16), field_shape),
+        in_specs=[scalar, scalar, scalar, vector],
+        out_specs=(vector, vector),
         scratch_shapes=[
             pltpu.VMEM((blocks, BLOCK, 48), bf16),
             pltpu.VMEM((blocks, 48, BLOCK), bf16),
             *work,
-            pltpu.SMEM((blocks + 8,), jnp.int32),
-            pltpu.SMEM((blocks + 8,), jnp.int32),
+            *[stage] * 4,
         ],
         compiler_params=limits,
-    )(core, pair_list, gathered)
+    )(core, count, pair_list, gathered)
     tiles = pltpu.with_memory_space_constraint(tiles, pltpu.VMEM)
     swap = [(place, place ^ 1) for place in range(col_devices)]
     state = None

time: 77.9 us -> 72.9 us (0.936)
  waiting for transfers between devices: 14.9 us -> 5.27 us
  Pallas kernels: 39.5 us -> 44.5 us
  blocking collectives: 10.4 us -> 13.2 us
  local copies, waits for them, and re-layouts: 3.76 us -> 1.43 us
    pallas_call x0 -> x2, Pallas kernels: none -> 10.8 us  [the longest x1 9.19 us: by_realizations(): pl.pallas_call(functools.partial(listing_kernel, plan, blocks), out_shape...]
    all_to_all x1, waiting for transfers between devices: 10.6 us -> 0.7 us  [by_realizations(): lax.all_to_all(outgoing, axes, 0, 0, tiled=True).reshape(blocks, 8, BLOCK)]
    pallas_call x1, Pallas kernels: 26.6 us -> 20.2 us  [by_realizations(): pl.pallas_call(functools.partial(first_kernel, plan), out_shape=(pltpu.VM...]
    all_to_all x1, blocking collectives: 10.4 us -> 13.2 us  [by_realizations(): received = lax.all_to_all(result, axes, 0, 0, tiled=True)]
    reshape x2 -> x0, local copies, waits for them, and re-layouts: 1.57 us -> none  [the longest x1 0.87 us: by_realizations(): right_side.reshape(chips, rows_here, blocks_here, BLOCK)]
  transfers between devices with their start and end apart: 4 -> 4, of which waited for: 4 -> 4; matrix products, arithmetic and copies ran while one was open for 0% -> 0% of each run, Pallas kernels for 0% -> 13%
where the time goes in v1:
time: 72.9 us; the launch traced here: 72.6 us
  Pallas kernels  44.5 us (61%)
  blocking collectives  13.2 us (18%)
  starting transfers between devices  7.52 us (10%)
  waiting for transfers between devices  5.27 us (7%)
  local copies, waits for them, and re-layouts  1.43 us (2%)
  between operations  0.74 us (1%)
    pallas_call x1, Pallas kernels, by_realizations(): pl.pallas_call(functools.partial(first_kernel, plan), out_shape=(pltpu.VM...  20.2 us
    all_to_all x1, blocking collectives, by_realizations(): received = lax.all_to_all(result, axes, 0, 0, tiled=True)  13.2 us
    pallas_call x2, Pallas kernels, by_realizations(): pl.pallas_call(functools.partial(next_kernel, first), out_shape=(field_sh...  13.2 us
    pallas_call x1, Pallas kernels, by_realizations(): pl.pallas_call(functools.partial(listing_kernel, plan, blocks), out_shape...  9.19 us
    all_to_all x1, starting transfers between devices, by_realizations(): lax.all_to_all(outgoing, axes, 0, 0, tiled=True).reshape(blocks, 8, BLOCK)  7.3 us
    ppermute x3, waiting for transfers between devices, by_realizations(): other = lax.ppermute(mine, 'col', swap)  4.57 us
    pallas_call x1, Pallas kernels, by_realizations(): pl.pallas_call(packing_kernel, out_shape=jax.ShapeDtypeStruct((devices, b...  1.6 us
  transfers between devices with their start and end apart: 4, of which 4 were waited for; matrix products, arithmetic and copies ran while one was open for 0% of the time, Pallas kernels for 13%

profile of v1, /device:TPU:0, one launch (start us, length us, event | category | flops | bytes accessed | tf_op | source)
XLA Modules:
  0.0 72.6 jit_solution(14694965023409507191)
XLA Ops:
  0.6 0.0 copy-start.1
  0.6 1.6 %shard_map.50 = f32[32,2,8,128]{3,2,1,0:T(8,128)} custom-call(f32[4,256]{1,0:T(4,128)} %point_hbm.1, f32[64,256]{1,0:T(8,128)} %field_hbm.1), custom_call_target="tpu_custom_call" | custom-call | tf_op jit(solution)/shard_map/pallas_call | solution.py:464
  2.2 7.3 %all-to-all-start = ((f32[32,2,8,128]{3,2,1,0:T(8,128)}), f32[32,2,8,128]{3,2,1,0:T(8,128)S(1)}, u32[]{:S(2)}, u32[]{:S(2)}) async-start(f32[32,2,8,128]{3,2,1,0:T(8,128)} %shard_map.50), calls=%async_computation | async-start | bytes 524288 | tf_op jit(solution)/shard_map/all_to_all | solution.py:492
  9.6 0.0 copy-start
  9.6 0.7 copy-done
  10.3 9.2 %shard_map.51 = (s32[192]{0:T(256)S(1)}, s32[744]{0:T(1024)S(1)}, s32[1]{0:T(128)}) custom-call(s32[1]{0:T(128)} %bitcast.core_ref, s32[2,468]{1,0:T(2,128)S(1)} %copy-done), custom_call_target="tpu_custom_call" | custom-call | flops 8000000000 | bytes 20000000 | tf_op jit(solution)/shard_map/pallas_call | solution.py:479
  19.5 0.7 all-to-all-done
  20.2 0.0 copy-done.1
  20.2 20.2 %shard_map.52 = (bf16[532,128,128]{2,1,0:T(8,128)(2,1)S(1)}, f32[64,8,128]{2,1,0:T(8,128)S(1)}) custom-call(s32[1]{0:T(128)} %bitcast.core_ref, s32[1]{0:T(128)} %get-tuple-element.13.count_ref, s32[2,468]{1,0:T(2,128)S(1)} %copy-done.1, f32[64,8,128]{2,1,0:T(8,128)S(1)} %bitcast.15), custom_call_target="tpu_custom_call" | custom-call | tf_op jit(solution)/shard_map/pallas_call | solution.py:498
  40.4 0.1 collective-permute-start
  40.5 1.5 %collective-permute-done.other_ref = f32[64,8,128]{2,1,0:T(8,128)S(1)} collective-permute-done((f32[64,8,128]{2,1,0:T(8,128)S(1)}, f32[64,8,128]{2,1,0:T(8,128)S(1)}, u32[]{:S(2)}, u32[]{:S(2)}) %collective-permute-start) | collective-permute-done | bytes 262176 | tf_op jit(solution)/shard_map/ppermute | solution.py:515
  42.0 6.6 %shard_map.53 = (f32[64,8,128]{2,1,0:T(8,128)S(1)}, f32[3,64,8,128]{3,2,1,0:T(8,128)S(1)}) custom-call(s32[192]{0:T(256)S(1)} %get-tuple-element.11.owner_ref, s32[744]{0:T(1024)S(1)} %get-tuple-element.12.entry_ref, s32[1]{0:T(128)} %get-tuple-element.13.count_ref, f32[64,8,128]{2,1,0:T(8,128)S(1)} %bitcast.16, ...), custom_call_target="tpu_custom_call" | custom-call | tf_op jit(solution)/shard_map/pallas_call | solution.py:518
  48.6 0.1 collective-permute-start.1
  48.7 1.5 %collective-permute-done.1.other_ref = f32[64,8,128]{2,1,0:T(8,128)S(1)} collective-permute-done((f32[64,8,128]{2,1,0:T(8,128)S(1)}, f32[64,8,128]{2,1,0:T(8,128)S(1)}, u32[]{:S(2)}, u32[]{:S(2)}) %collective-permute-start.1) | collective-permute-done | bytes 262176 | tf_op jit(solution)/shard_map/ppermute | solution.py:515
  50.2 6.6 %shard_map.54 = (f32[64,8,128]{2,1,0:T(8,128)S(1)}, f32[3,64,8,128]{3,2,1,0:T(8,128)S(1)}) custom-call(s32[192]{0:T(256)S(1)} %get-tuple-element.11.owner_ref, s32[744]{0:T(1024)S(1)} %get-tuple-element.12.entry_ref, s32[1]{0:T(128)} %get-tuple-element.13.count_ref, f32[64,8,128]{2,1,0:T(8,128)S(1)} %bitcast.17, ...), custom_call_target="tpu_custom_call" | custom-call | tf_op jit(solution)/shard_map/pallas_call | solution.py:518
  56.8 0.1 collective-permute-start.2
  56.9 1.5 %collective-permute-done.2.other_ref = f32[64,8,128]{2,1,0:T(8,128)S(1)} collective-permute-done((f32[64,8,128]{2,1,0:T(8,128)S(1)}, f32[64,8,128]{2,1,0:T(8,128)S(1)}, u32[]{:S(2)}, u32[]{:S(2)}) %collective-permute-start.2) | collective-permute-done | bytes 262176 | tf_op jit(solution)/shard_map/ppermute | solution.py:526
  58.4 0.3 shard_map.55
  58.7 13.2 %all_to_all.10 = f32[32,2,4,128]{3,2,1,0:T(4,128)S(1)} all-to-all(f32[32,2,4,128]{3,2,1,0:T(4,128)S(1)} %bitcast.19), channel_id=1, replica_groups=mesh['row'=4,'col'=8] {'row','col'}, dimensions={0} | all-to-all | bytes 262144 | tf_op jit(solution)/shard_map/all_to_all | solution.py:535
  71.8 0.1 copy.11
  71.9 0.7 copy_bitcast_fusion.1
  (1 shorter events, 0.0 us)
Async XLA Ops:
  0.6 19.5 %copy-start.1 = (s32[2,468]{1,0:T(2,128)S(1)}, s32[2,468]{1,0:T(2,128)}, u32[]{:S(2)}) copy-start(s32[2,468]{1,0:T(2,128)} %pair_ref.3) | copy-start | bytes 11236
  2.2 17.9 %all-to-all-start = ((f32[32,2,8,128]{3,2,1,0:T(8,128)}), f32[32,2,8,128]{3,2,1,0:T(8,128)S(1)}, u32[]{:S(2)}, u32[]{:S(2)}) async-start(f32[32,2,8,128]{3,2,1,0:T(8,128)} %shard_map.50), calls=%async_computation | async-start | bytes 524288 | tf_op jit(solution)/shard_map/all_to_all | solution.py:492
  9.6 0.7 copy-start
  40.4 1.6 %collective-permute-start = (f32[64,8,128]{2,1,0:T(8,128)S(1)}, f32[64,8,128]{2,1,0:T(8,128)S(1)}, u32[]{:S(2)}, u32[]{:S(2)}) collective-permute-start(f32[64,8,128]{2,1,0:T(8,128)S(1)} %get-tuple-element.14.mine_ref), channel_id=1, source_target_pairs={{0,1},{1,0},{2,3},{3,2},{4,5},{5,4},{6,7},{7,6},{8,9},{9,8},{10,11... | collective-permute-start | bytes 786440 | tf_op jit(solution)/shard_map/ppermute | solution.py:515
  48.6 1.6 %collective-permute-start.1 = (f32[64,8,128]{2,1,0:T(8,128)S(1)}, f32[64,8,128]{2,1,0:T(8,128)S(1)}, u32[]{:S(2)}, u32[]{:S(2)}) collective-permute-start(f32[64,8,128]{2,1,0:T(8,128)S(1)} %get-tuple-element.16.mine_ref), channel_id=1, source_target_pairs={{0,1},{1,0},{2,3},{3,2},{4,5},{5,4},{6,7},{7,6},{8,9},{9,8},{10,11... | collective-permute-start | bytes 786440 | tf_op jit(solution)/shard_map/ppermute | solution.py:515
  56.8 1.6 %collective-permute-start.2 = (f32[64,8,128]{2,1,0:T(8,128)S(1)}, f32[64,8,128]{2,1,0:T(8,128)S(1)}, u32[]{:S(2)}, u32[]{:S(2)}) collective-permute-start(f32[64,8,128]{2,1,0:T(8,128)S(1)} %get-tuple-element.18.mine_ref), channel_id=1, source_target_pairs={{0,1},{1,0},{2,3},{3,2},{4,5},{5,4},{6,7},{7,6},{8,9},{9,8},{10,11... | collective-permute-start | bytes 786440 | tf_op jit(solution)/shard_map/ppermute | solution.py:526

commit v2 on v1

--- a/solution.py
+++ b/solution.py
@@ -15,8 +15,9 @@
 nugget = 1.0
 tiles_per_step = 8
 rows_here = 4
-chunk = 4
-chunks_per_step = 8
+chunk_bits = 2
+chunk = 1 << chunk_bits
+chunks_per_step = 16
 tile_bytes_limit = 24 * 2**20
 kernel_bytes = 12 * 2**20
 f32 = jnp.float32
@@ -205,64 +206,62 @@
     return low, high, usable, pair_usable
 
 
-def listing_kernel(
-    plan, blocks, core_ref, pair_ref, owner_ref, entry_ref, count_ref, length_ref, open_ref
-):
-    _, width, steps, chunks = plan
+def listing_kernel(plan, blocks, core_ref, pair_ref, owner_ref, entry_ref, count_ref, open_ref):
+    half, width, steps, chunks = plan
+    listed = pair_ref.shape[1]
     core = core_ref[0]
     slots = width * steps
-    spare = chunks * chunk
-    empty = blocks
 
     def clear(block, carry):
-        length_ref[block] = 0
         open_ref[block] = 0
         return carry
 
-    lax.fori_loop(0, blocks + 1, clear, 0)
-
-    def append(block, entry, usable, used):
-        length = length_ref[block]
-        place = length & (chunk - 1)
-        fresh = place == 0
-        where = jnp.where(fresh, used, open_ref[block])
-        begins = fresh & usable
-        target = jnp.where(usable, block, blocks)
-        length_ref[target] = length + 1
-        open_ref[target] = where
-        for slot in range(1, chunk):
-            entry_ref[jnp.where(begins, where * chunk + slot, spare)] = empty
-        entry_ref[jnp.where(usable, where * chunk + place, spare)] = entry
-        owner_ref[jnp.where(usable, where, chunks)] = block
-        return used + begins.astype(jnp.int32)
-
-    def list_tiles(step, used):
-        for slot in range(width):
-            number = step * width + slot
-            low, high, usable, pair_usable = entry_blocks(plan, blocks, core, pair_ref, number)
-            used = append(high, number * 65536 + low, usable, used)
-            used = append(low, (slots + number) * 65536 + high, pair_usable, used)
-        return used
-
-    used = lax.fori_loop(0, steps, list_tiles, 0)
+    def pad(place, carry):
+        entry_ref[place] = blocks
+        return carry
+
+    lax.fori_loop(0, blocks, clear, 0, unroll=16)
+    lax.fori_loop(0, chunks * chunk, pad, 0, unroll=16)
+
+    def append(block, entry, used):
+        place = open_ref[block]
+        fresh = (place & (chunk - 1)) == 0
+        place = jnp.where(fresh, used, place)
+        open_ref[block] = place + 1
+        entry_ref[place] = entry
+        owner_ref[place >> chunk_bits] = block
+        return jnp.where(fresh, used + chunk, used)
+
+    def list_pair(number, used):
+        low = pair_ref[0, core * half + number]
+        high = pair_ref[1, core * half + number]
+        used = append(high, number * 65536 + low, used)
+        return append(low, (slots + number) * 65536 + high, used)
+
+    def list_diagonal(number, used):
+        block = core * (blocks // 2) + number
+        return append(block, (half + number) * 65536 + block, used)
+
+    used = lax.fori_loop(0, listed // 2, list_pair, 0, unroll=8)
+    if listed % 2:
+        used = lax.fori_loop(half - 1, half - core, list_pair, used)
+    used = lax.fori_loop(0, blocks // 2, list_diagonal, used, unroll=8)
+    used = used >> chunk_bits
     count_ref[0] = used
     for part in range(chunks_per_step):
         owner_ref[used + part] = blocks
-        for slot in range(chunk):
-            entry_ref[(used + part) * chunk + slot] = empty
 
 
 def radial(squared):
     squared = jnp.maximum(squared, 1e-30)
     distance = squared * lax.rsqrt(squared)
-    near = jnp.maximum(long_range - distance, 0.0)
-    close = jnp.maximum(short_range - distance, 0.0)
-
-    def falling(remain, reach):
-        square = remain * remain
-        return square * square * (5.0 / reach**4 - 4.0 / reach**5 * remain)
-
-    return (falling(near, long_range) + falling(close, short_range)).astype(bf16)
+    near = jnp.maximum(1.0 - distance * (1.0 / long_range), 0.0)
+    near_square = near * near
+    wide = near_square * near_square * (1.25 - near)
+    close = jnp.maximum(1.0 - distance * (1.0 / short_range), 0.0).astype(bf16)
+    close_square = close * close
+    narrow = close_square * close_square * (jnp.asarray(1.25, bf16) - close)
+    return wide.astype(bf16) + narrow
 
 
 def three_parts(values):
@@ -277,7 +276,7 @@
 
 
 def store_scaled(fields_ref, direction, scale):
-    scaled = jnp.where(row_number(direction.shape) < rows_here, direction * scale, 0.0)
+    scaled = jnp.where(row_number(direction.shape) < rows_here, direction * (4.0 * scale), 0.0)
     blocks = direction.shape[0]
     doubled = jnp.concatenate([scaled, jnp.zeros_like(scaled)], axis=1)
     fields_ref[0:blocks] = doubled.astype(bf16)
@@ -350,42 +349,55 @@
     store_scaled(fields_ref, gathered_ref[...], gathered_ref[:, 7:8, :])
     totals_ref[...] = jnp.zeros_like(totals_ref)
 
-    def make_tiles(step, stage):
-        for slot in range(width):
-            number = step * width + slot
-            low, high, _, _ = entry_blocks(plan, blocks, core, pair_ref, number)
-            squared = jnp.dot(left_ref[low], right_ref[high], preferred_element_type=f32)
-            tile = radial(squared)
-            turned = tile.T
-            tiles_ref[number] = tile
-            tiles_ref[slots + number] = turned
-            stage[0][slot] = tile
-            stage[1][slot] = turned
-
-    def use_tiles(step, stage):
+    def make_tile(step, slot, stage):
+        number = step * width + slot
+        low, high, _, _ = entry_blocks(plan, blocks, core, pair_ref, number)
+        squared = jnp.dot(left_ref[low], right_ref[high], preferred_element_type=f32)
+        tile = radial(squared)
+        turned = tile.T
+        tiles_ref[number] = tile
+        tiles_ref[slots + number] = turned
+        stage[0][slot] = tile
+        stage[1][slot] = turned
+
+    def use_tile(step, slot, stage):
+        number = step * width + slot
+        low, high, usable, pair_usable = entry_blocks(plan, blocks, core, pair_ref, number)
+        usable = usable & (number >= 0)
+        pair_usable = pair_usable & (number >= 0)
+        ways = (
+            (jnp.where(usable, low, blocks), jnp.where(usable, high, blocks)),
+            (jnp.where(pair_usable, high, blocks), jnp.where(pair_usable, low, blocks)),
+        )
         products = []
-        for slot in range(width):
-            number = step * width + slot
-            low, high, usable, pair_usable = entry_blocks(plan, blocks, core, pair_ref, number)
-            usable = usable & (number >= 0)
-            pair_usable = pair_usable & (number >= 0)
-            ways = (
-                (jnp.where(usable, low, blocks), jnp.where(usable, high, blocks)),
-                (jnp.where(pair_usable, high, blocks), jnp.where(pair_usable, low, blocks)),
-            )
-            for (source, target), tiles in zip(ways, stage):
-                product = jnp.dot(fields_ref[source], tiles[slot], preferred_element_type=f32)
-                products.append((target, product[0:8]))
+        for (source, target), tiles in zip(ways, stage):
+            product = jnp.dot(fields_ref[source], tiles[slot], preferred_element_type=f32)
+            products.append((target, product[0:8]))
+        return products
+
+    def add_products(products):
         for target, product in products:
             totals_ref[target] += product
 
+    def use_tiles(step, stage):
+        for slot in range(width):
+            add_products(use_tile(step, slot, stage))
+
+    def both(step, new_stage, old_stage):
+        waiting = []
+        for slot in range(width):
+            make_tile(step, slot, new_stage)
+            waiting.append(use_tile(step - 1, slot, old_stage))
+            if len(waiting) > 2:
+                add_products(waiting.pop(0))
+        for products in waiting:
+            add_products(products)
+
     even, odd = stages[0:2], stages[2:4]
 
     def both_steps(pair, carry):
-        make_tiles(2 * pair, even)
-        use_tiles(2 * pair - 1, odd)
-        make_tiles(2 * pair + 1, odd)
-        use_tiles(2 * pair, even)
+        both(2 * pair, even, odd)
+        both(2 * pair + 1, odd, even)
         return carry
 
     lax.fori_loop(0, steps // 2, both_steps, 0)
@@ -485,7 +497,7 @@
         ),
         in_specs=[scalar, scalar],
         out_specs=(scalar, scalar, scalar),
-        scratch_shapes=[pltpu.SMEM((blocks + 8,), jnp.int32)] * 2,
+        scratch_shapes=[pltpu.SMEM((blocks,), jnp.int32)],
         cost_estimate=pl.CostEstimate(flops=8_000_000_000, bytes_accessed=20_000_000, transcendentals=0),
         compiler_params=limits,
     )(core, pair_list)

time: 72.9 us -> 65 us (0.89)
  Pallas kernels: 44.5 us -> 36.3 us
  waiting for transfers between devices: 5.27 us -> 8.3 us
  blocking collectives: 13.2 us -> 10.4 us
    pallas_call x1, Pallas kernels: 20.2 us -> 16.9 us  [by_realizations(): pl.pallas_call(functools.partial(first_kernel, plan), out_shape=(pltpu.VM...]
    all_to_all x1, waiting for transfers between devices: 0.7 us -> 3.73 us  [by_realizations(): lax.all_to_all(outgoing, axes, 0, 0, tiled=True).reshape(blocks, 8, BLOCK)]
    pallas_call x1, Pallas kernels: 9.19 us -> 6.17 us  [by_realizations(): pl.pallas_call(functools.partial(listing_kernel, plan, blocks), out_shape...]
    all_to_all x1, blocking collectives: 13.2 us -> 10.4 us  [by_realizations(): received = lax.all_to_all(result, axes, 0, 0, tiled=True)]
    pallas_call x2, Pallas kernels: 13.2 us -> 11.3 us  [by_realizations(): pl.pallas_call(functools.partial(next_kernel, first), out_shape=(field_sh...]
  transfers between devices with their start and end apart: 4 -> 4, of which waited for: 4 -> 4; matrix products, arithmetic and copies ran while one was open for 0% -> 0% of each run, Pallas kernels for 13% -> 10%
where the time goes in v2:
time: 65 us; the launch traced here: 64.7 us
  Pallas kernels  36.3 us (56%)
  blocking collectives  10.4 us (16%)
  waiting for transfers between devices  8.3 us (13%)
  starting transfers between devices  7.52 us (12%)
  local copies, waits for them, and re-layouts  1.43 us (2%)
  between operations  0.74 us (1%)
    pallas_call x1, Pallas kernels, by_realizations(): pl.pallas_call(functools.partial(first_kernel, plan), out_shape=(pltpu.VM...  16.9 us
    pallas_call x2, Pallas kernels, by_realizations(): pl.pallas_call(functools.partial(next_kernel, first), out_shape=(field_sh...  11.3 us
    all_to_all x1, blocking collectives, by_realizations(): received = lax.all_to_all(result, axes, 0, 0, tiled=True)  10.4 us
    all_to_all x1, starting transfers between devices, by_realizations(): lax.all_to_all(outgoing, axes, 0, 0, tiled=True).reshape(blocks, 8, BLOCK)  7.3 us
    pallas_call x1, Pallas kernels, by_realizations(): pl.pallas_call(functools.partial(listing_kernel, plan, blocks), out_shape...  6.17 us
    ppermute x3, waiting for transfers between devices, by_realizations(): other = lax.ppermute(mine, 'col', swap)  4.57 us
    all_to_all x1, waiting for transfers between devices, by_realizations(): lax.all_to_all(outgoing, axes, 0, 0, tiled=True).reshape(blocks, 8, BLOCK)  3.73 us
    pallas_call x1, Pallas kernels, by_realizations(): pl.pallas_call(packing_kernel, out_shape=jax.ShapeDtypeStruct((devices, b...  1.6 us
  transfers between devices with their start and end apart: 4, of which 4 were waited for; matrix products, arithmetic and copies ran while one was open for 0% of the time, Pallas kernels for 10%

profile of v2, /device:TPU:0, one launch (start us, length us, event | category | flops | bytes accessed | tf_op | source)
XLA Modules:
  0.0 64.7 jit_solution(1162949121888301386)
XLA Ops:
  0.6 0.0 copy-start.1
  0.6 1.6 %shard_map.50 = f32[32,2,8,128]{3,2,1,0:T(8,128)} custom-call(f32[4,256]{1,0:T(4,128)} %point_hbm.1, f32[64,256]{1,0:T(8,128)} %field_hbm.1), custom_call_target="tpu_custom_call" | custom-call | tf_op jit(solution)/shard_map/pallas_call | solution.py:476
  2.2 7.3 %all-to-all-start = ((f32[32,2,8,128]{3,2,1,0:T(8,128)}), f32[32,2,8,128]{3,2,1,0:T(8,128)S(1)}, u32[]{:S(2)}, u32[]{:S(2)}) async-start(f32[32,2,8,128]{3,2,1,0:T(8,128)} %shard_map.50), calls=%async_computation | async-start | bytes 524288 | tf_op jit(solution)/shard_map/all_to_all | solution.py:504
  9.6 0.0 copy-start
  9.6 0.7 %copy-done = s32[2,468]{1,0:T(2,128)S(1)} copy-done((s32[2,468]{1,0:T(2,128)S(1)}, s32[2,468]{1,0:T(2,128)}, u32[]{:S(2)}) %copy-start) | copy-done | bytes 3768
  10.3 6.2 %shard_map.51 = (s32[200]{0:T(256)S(1)}, s32[776]{0:T(1024)S(1)}, s32[1]{0:T(128)}) custom-call(s32[1]{0:T(128)} %bitcast.core_ref, s32[2,468]{1,0:T(2,128)S(1)} %copy-done), custom_call_target="tpu_custom_call" | custom-call | flops 8000000000 | bytes 20000000 | tf_op jit(solution)/shard_map/pallas_call | solution.py:491
  16.4 3.7 %all-to-all-done = f32[32,2,8,128]{3,2,1,0:T(8,128)S(1)} async-done(((f32[32,2,8,128]{3,2,1,0:T(8,128)}), f32[32,2,8,128]{3,2,1,0:T(8,128)S(1)}, u32[]{:S(2)}, u32[]{:S(2)}) %all-to-all-start) | async-done | bytes 262176 | tf_op jit(solution)/shard_map/all_to_all | solution.py:504
  20.2 0.0 copy-done.1
  20.2 16.9 %shard_map.52 = (bf16[532,128,128]{2,1,0:T(8,128)(2,1)S(1)}, f32[64,8,128]{2,1,0:T(8,128)S(1)}) custom-call(s32[1]{0:T(128)} %bitcast.core_ref, s32[1]{0:T(128)} %get-tuple-element.13.count_ref, s32[2,468]{1,0:T(2,128)S(1)} %copy-done.1, f32[64,8,128]{2,1,0:T(8,128)S(1)} %bitcast.15), custom_call_target="tpu_custom_call" | custom-call | tf_op jit(solution)/shard_map/pallas_call | solution.py:510
  37.1 0.1 collective-permute-start
  37.1 1.5 %collective-permute-done.other_ref = f32[64,8,128]{2,1,0:T(8,128)S(1)} collective-permute-done((f32[64,8,128]{2,1,0:T(8,128)S(1)}, f32[64,8,128]{2,1,0:T(8,128)S(1)}, u32[]{:S(2)}, u32[]{:S(2)}) %collective-permute-start) | collective-permute-done | bytes 262176 | tf_op jit(solution)/shard_map/ppermute | solution.py:527
  38.7 5.7 %shard_map.53 = (f32[64,8,128]{2,1,0:T(8,128)S(1)}, f32[3,64,8,128]{3,2,1,0:T(8,128)S(1)}) custom-call(s32[200]{0:T(256)S(1)} %get-tuple-element.11.owner_ref, s32[776]{0:T(1024)S(1)} %get-tuple-element.12.entry_ref, s32[1]{0:T(128)} %get-tuple-element.13.count_ref, f32[64,8,128]{2,1,0:T(8,128)S(1)} %bitcast.16, ...), custom_call_target="tpu_custom_call" | custom-call | tf_op jit(solution)/shard_map/pallas_call | solution.py:530
  44.4 0.1 collective-permute-start.1
  44.4 1.5 %collective-permute-done.1.other_ref = f32[64,8,128]{2,1,0:T(8,128)S(1)} collective-permute-done((f32[64,8,128]{2,1,0:T(8,128)S(1)}, f32[64,8,128]{2,1,0:T(8,128)S(1)}, u32[]{:S(2)}, u32[]{:S(2)}) %collective-permute-start.1) | collective-permute-done | bytes 262176 | tf_op jit(solution)/shard_map/ppermute | solution.py:527
  46.0 5.7 %shard_map.54 = (f32[64,8,128]{2,1,0:T(8,128)S(1)}, f32[3,64,8,128]{3,2,1,0:T(8,128)S(1)}) custom-call(s32[200]{0:T(256)S(1)} %get-tuple-element.11.owner_ref, s32[776]{0:T(1024)S(1)} %get-tuple-element.12.entry_ref, s32[1]{0:T(128)} %get-tuple-element.13.count_ref, f32[64,8,128]{2,1,0:T(8,128)S(1)} %bitcast.17, ...), custom_call_target="tpu_custom_call" | custom-call | tf_op jit(solution)/shard_map/pallas_call | solution.py:530
  51.6 0.1 collective-permute-start.2
  51.7 1.5 %collective-permute-done.2.other_ref = f32[64,8,128]{2,1,0:T(8,128)S(1)} collective-permute-done((f32[64,8,128]{2,1,0:T(8,128)S(1)}, f32[64,8,128]{2,1,0:T(8,128)S(1)}, u32[]{:S(2)}, u32[]{:S(2)}) %collective-permute-start.2) | collective-permute-done | bytes 262176 | tf_op jit(solution)/shard_map/ppermute | solution.py:538
  53.2 0.3 shard_map.55
  53.5 10.4 %all_to_all.10 = f32[32,2,4,128]{3,2,1,0:T(4,128)S(1)} all-to-all(f32[32,2,4,128]{3,2,1,0:T(4,128)S(1)} %bitcast.19), channel_id=1, replica_groups=mesh['row'=4,'col'=8] {'row','col'}, dimensions={0} | all-to-all | bytes 262144 | tf_op jit(solution)/shard_map/all_to_all | solution.py:547
  64.0 0.1 copy.11
  64.0 0.7 %copy_bitcast_fusion.1 = (f32[64,256]{1,0:T(8,128)}, f32[64,256]{1,0:T(8,128)}) fusion(f32[8,8,2,128]{3,2,1,0:T(2,128)S(1)} %bitcast.22, f32[8,8,2,128]{3,2,1,0:T(2,128)S(1)} %bitcast.23), kind=kLoop, calls=%fused_computation.1 | loop fusion | bytes 262144 | tf_op jit(solution)/shard_map/squeeze | solution.py:550
  (1 shorter events, 0.0 us)
Async XLA Ops:
  0.6 19.5 %copy-start.1 = (s32[2,468]{1,0:T(2,128)S(1)}, s32[2,468]{1,0:T(2,128)}, u32[]{:S(2)}) copy-start(s32[2,468]{1,0:T(2,128)} %pair_ref.3) | copy-start | bytes 11236
  2.2 17.9 %all-to-all-start = ((f32[32,2,8,128]{3,2,1,0:T(8,128)}), f32[32,2,8,128]{3,2,1,0:T(8,128)S(1)}, u32[]{:S(2)}, u32[]{:S(2)}) async-start(f32[32,2,8,128]{3,2,1,0:T(8,128)} %shard_map.50), calls=%async_computation | async-start | bytes 524288 | tf_op jit(solution)/shard_map/all_to_all | solution.py:504
  9.6 0.7 %copy-start = (s32[2,468]{1,0:T(2,128)S(1)}, s32[2,468]{1,0:T(2,128)}, u32[]{:S(2)}) copy-start(s32[2,468]{1,0:T(2,128)} %pair_ref.3) | copy-start | bytes 11236
  37.1 1.6 %collective-permute-start = (f32[64,8,128]{2,1,0:T(8,128)S(1)}, f32[64,8,128]{2,1,0:T(8,128)S(1)}, u32[]{:S(2)}, u32[]{:S(2)}) collective-permute-start(f32[64,8,128]{2,1,0:T(8,128)S(1)} %get-tuple-element.14.mine_ref), channel_id=1, source_target_pairs={{0,1},{1,0},{2,3},{3,2},{4,5},{5,4},{6,7},{7,6},{8,9},{9,8},{10,11... | collective-permute-start | bytes 786440 | tf_op jit(solution)/shard_map/ppermute | solution.py:527
  44.4 1.6 %collective-permute-start.1 = (f32[64,8,128]{2,1,0:T(8,128)S(1)}, f32[64,8,128]{2,1,0:T(8,128)S(1)}, u32[]{:S(2)}, u32[]{:S(2)}) collective-permute-start(f32[64,8,128]{2,1,0:T(8,128)S(1)} %get-tuple-element.16.mine_ref), channel_id=1, source_target_pairs={{0,1},{1,0},{2,3},{3,2},{4,5},{5,4},{6,7},{7,6},{8,9},{9,8},{10,11... | collective-permute-start | bytes 786440 | tf_op jit(solution)/shard_map/ppermute | solution.py:527
  51.6 1.6 %collective-permute-start.2 = (f32[64,8,128]{2,1,0:T(8,128)S(1)}, f32[64,8,128]{2,1,0:T(8,128)S(1)}, u32[]{:S(2)}, u32[]{:S(2)}) collective-permute-start(f32[64,8,128]{2,1,0:T(8,128)S(1)} %get-tuple-element.18.mine_ref), channel_id=1, source_target_pairs={{0,1},{1,0},{2,3},{3,2},{4,5},{5,4},{6,7},{7,6},{8,9},{9,8},{10,11... | collective-permute-start | bytes 786440 | tf_op jit(solution)/shard_map/ppermute | solution.py:538

commit v3 on v2

--- a/solution.py
+++ b/solution.py
@@ -17,7 +17,7 @@
 rows_here = 4
 chunk_bits = 2
 chunk = 1 << chunk_bits
-chunks_per_step = 16
+chunks_per_step = 32
 tile_bytes_limit = 24 * 2**20
 kernel_bytes = 12 * 2**20
 f32 = jnp.float32
@@ -192,21 +192,18 @@
             outgoing_ref[2 * chip + 1, block] = both
 
 
-def entry_blocks(plan, blocks, core, pair_ref, number):
-    half = plan[0]
-    listed = pair_ref.shape[1]
-    pair = core * half + number
-    is_pair = number < half
-    pair_usable = is_pair & (pair < listed)
-    usable = pair_usable | ((number >= half) & (number < half + blocks // 2))
-    safe = jnp.minimum(pair, listed - 1)
-    own = jnp.minimum(core * (blocks // 2) + number - half, blocks - 1)
-    low = jnp.where(is_pair, pair_ref[0, safe], own)
-    high = jnp.where(is_pair, pair_ref[1, safe], own)
-    return low, high, usable, pair_usable
-
-
-def listing_kernel(plan, blocks, core_ref, pair_ref, owner_ref, entry_ref, count_ref, open_ref):
+def listing_kernel(
+    plan,
+    blocks,
+    core_ref,
+    pair_ref,
+    owner_ref,
+    entry_ref,
+    count_ref,
+    low_ref,
+    high_ref,
+    open_ref,
+):
     half, width, steps, chunks = plan
     listed = pair_ref.shape[1]
     core = core_ref[0]
@@ -235,13 +232,22 @@
     def list_pair(number, used):
         low = pair_ref[0, core * half + number]
         high = pair_ref[1, core * half + number]
+        low_ref[number] = low
+        high_ref[number] = high
         used = append(high, number * 65536 + low, used)
         return append(low, (slots + number) * 65536 + high, used)
 
     def list_diagonal(number, used):
         block = core * (blocks // 2) + number
+        low_ref[half + number] = block
+        high_ref[half + number] = block
         return append(block, (half + number) * 65536 + block, used)
 
+    low_ref[half - 1] = blocks
+    high_ref[half - 1] = blocks
+    for number in range(half + blocks // 2, slots):
+        low_ref[number] = blocks
+        high_ref[number] = blocks
     used = lax.fori_loop(0, listed // 2, list_pair, 0, unroll=8)
     if listed % 2:
         used = lax.fori_loop(half - 1, half - core, list_pair, used)
@@ -310,9 +316,8 @@
 
 def first_kernel(
     plan,
-    core_ref,
-    count_ref,
-    pair_ref,
+    low_ref,
+    high_ref,
     gathered_ref,
     tiles_ref,
     product_ref,
@@ -322,9 +327,8 @@
     totals_ref,
     *stages,
 ):
-    _, width, steps, _ = plan
+    half, width, steps, _ = plan
     blocks = gathered_ref.shape[0]
-    core = core_ref[0]
     slots = width * steps
     highest = jnp.max(jnp.max(gathered_ref[...], axis=0), axis=1, keepdims=True)
     lowest = jnp.min(jnp.min(gathered_ref[...], axis=0), axis=1, keepdims=True)
@@ -346,13 +350,19 @@
         return carry
 
     lax.fori_loop(0, blocks, prepare, 0, unroll=8)
+    left_ref[blocks] = jnp.zeros((BLOCK, 48), bf16)
+    right_ref[blocks] = jnp.zeros((48, BLOCK), bf16)
     store_scaled(fields_ref, gathered_ref[...], gathered_ref[:, 7:8, :])
     totals_ref[...] = jnp.zeros_like(totals_ref)
 
-    def make_tile(step, slot, stage):
+    def square(step, slot):
         number = step * width + slot
-        low, high, _, _ = entry_blocks(plan, blocks, core, pair_ref, number)
-        squared = jnp.dot(left_ref[low], right_ref[high], preferred_element_type=f32)
+        return jnp.dot(
+            left_ref[low_ref[number]], right_ref[high_ref[number]], preferred_element_type=f32
+        )
+
+    def make_tile(step, slot, stage, squared):
+        number = step * width + slot
         tile = radial(squared)
         turned = tile.T
         tiles_ref[number] = tile
@@ -362,12 +372,13 @@
 
     def use_tile(step, slot, stage):
         number = step * width + slot
-        low, high, usable, pair_usable = entry_blocks(plan, blocks, core, pair_ref, number)
-        usable = usable & (number >= 0)
-        pair_usable = pair_usable & (number >= 0)
+        made = jnp.maximum(number, 0)
+        low = jnp.where(number >= 0, low_ref[made], blocks)
+        high = jnp.where(number >= 0, high_ref[made], blocks)
+        is_pair = number < half
         ways = (
-            (jnp.where(usable, low, blocks), jnp.where(usable, high, blocks)),
-            (jnp.where(pair_usable, high, blocks), jnp.where(pair_usable, low, blocks)),
+            (low, high),
+            (jnp.where(is_pair, high, blocks), jnp.where(is_pair, low, blocks)),
         )
         products = []
         for (source, target), tiles in zip(ways, stage):
@@ -385,8 +396,12 @@
 
     def both(step, new_stage, old_stage):
         waiting = []
+        ahead = square(step, 0)
         for slot in range(width):
-            make_tile(step, slot, new_stage)
+            squared = ahead
+            if slot + 1 < width:
+                ahead = square(step, slot + 1)
+            make_tile(step, slot, new_stage, squared)
             waiting.append(use_tile(step - 1, slot, old_stage))
             if len(waiting) > 2:
                 add_products(waiting.pop(0))
@@ -455,7 +470,7 @@
     scale = gathered_ref[:, 7:8, :]
     moved, residual, _ = advance(mine_ref, other_ref, scale, state_ref[2], state_ref[1])
     chosen = jnp.where(core_ref[0] == 0, state_ref[0] + moved, residual)
-    result_ref[...] = chosen[:, 0:rows_here, :]
+    result_ref[...] = chosen[:, 0:rows_here, :].astype(bf16)
 
 
 def by_realizations(point_data, right_side, pair_list):
@@ -488,19 +503,21 @@
         pltpu.with_memory_space_constraint(point_data, pltpu.HBM),
         pltpu.with_memory_space_constraint(right_side, pltpu.HBM),
     )
-    owner, entry, count = pl.pallas_call(
+    owner, entry, count, low, high = pl.pallas_call(
         functools.partial(listing_kernel, plan, blocks),
         out_shape=(
-            jax.ShapeDtypeStruct((chunks + 8,), jnp.int32),
-            jax.ShapeDtypeStruct((chunks * chunk + 8,), jnp.int32),
-            jax.ShapeDtypeStruct((1,), jnp.int32),
+            pltpu.SMEM((chunks + 8,), jnp.int32),
+            pltpu.SMEM((chunks * chunk + 8,), jnp.int32),
+            pltpu.SMEM((1,), jnp.int32),
+            pltpu.SMEM((slots,), jnp.int32),
+            pltpu.SMEM((slots,), jnp.int32),
         ),
         in_specs=[scalar, scalar],
-        out_specs=(scalar, scalar, scalar),
+        out_specs=(scalar,) * 5,
         scratch_shapes=[pltpu.SMEM((blocks,), jnp.int32)],
         cost_estimate=pl.CostEstimate(flops=8_000_000_000, bytes_accessed=20_000_000, transcendentals=0),
         compiler_params=limits,
-    )(core, pair_list)
+    )(core, pltpu.with_memory_space_constraint(pair_list, pltpu.HBM))
     gathered = lax.all_to_all(outgoing, axes, 0, 0, tiled=True).reshape(blocks, 8, BLOCK)
 
     field_shape = jax.ShapeDtypeStruct((blocks, 8, BLOCK), f32)
@@ -510,16 +527,16 @@
     tiles, mine = pl.pallas_call(
         functools.partial(first_kernel, plan),
         out_shape=(pltpu.VMEM((2 * slots, BLOCK, BLOCK), bf16), field_shape),
-        in_specs=[scalar, scalar, scalar, vector],
+        in_specs=[scalar, scalar, vector],
         out_specs=(vector, vector),
         scratch_shapes=[
-            pltpu.VMEM((blocks, BLOCK, 48), bf16),
-            pltpu.VMEM((blocks, 48, BLOCK), bf16),
+            pltpu.VMEM((blocks + 1, BLOCK, 48), bf16),
+            pltpu.VMEM((blocks + 1, 48, BLOCK), bf16),
             *work,
             *[stage] * 4,
         ],
         compiler_params=limits,
-    )(core, count, pair_list, gathered)
+    )(low, high, gathered)
     tiles = pltpu.with_memory_space_constraint(tiles, pltpu.VMEM)
     swap = [(place, place ^ 1) for place in range(col_devices)]
     state = None
@@ -538,7 +555,7 @@
     other = lax.ppermute(mine, "col", swap)
     result = pl.pallas_call(
         last_kernel,
-        out_shape=jax.ShapeDtypeStruct((blocks, rows_here, BLOCK), f32),
+        out_shape=jax.ShapeDtypeStruct((blocks, rows_here, BLOCK), bf16),
         in_specs=[scalar] + [vector] * 4,
         out_specs=vector,
         compiler_params=limits,
@@ -547,7 +564,7 @@
     received = lax.all_to_all(result, axes, 0, 0, tiled=True)
     received = received.reshape(chips, 2, blocks_here, rows_here, BLOCK)
     received = received.transpose(1, 0, 3, 2, 4).reshape(2, right_side.shape[0], -1)
-    return received[0], received[1]
+    return received[0].astype(f32), received[1].astype(f32)
 
 
 def per_device(point_data, right_side, pair_list):

time: 65 us -> 58.4 us (0.90)
  Pallas kernels: 36.3 us -> 30.2 us
  blocking collectives: 10.4 us -> 9.62 us
  local copies, waits for them, and re-layouts: 1.43 us -> 0.71 us
  waiting for transfers between devices: 8.3 us -> 8.97 us
    pallas_call x2, Pallas kernels: 11.3 us -> 7.61 us  [by_realizations(): pl.pallas_call(functools.partial(next_kernel, first), out_shape=(field_sh...]
    pallas_call x1, Pallas kernels: 16.9 us -> 14.8 us  [by_realizations(): pl.pallas_call(functools.partial(first_kernel, plan), out_shape=(pltpu.VM...]
    all_to_all x1, waiting for transfers between devices: 3.73 us -> 4.69 us  [by_realizations(): lax.all_to_all(outgoing, axes, 0, 0, tiled=True).reshape(blocks, 8, BLOCK)]
    all_to_all x1, blocking collectives: 10.4 us -> 9.62 us  [by_realizations(): received = lax.all_to_all(result, axes, 0, 0, tiled=True)]
    unnamed x4 -> x0, local copies, waits for them, and re-layouts: 0.69 us -> none
    convert_element_type x0 -> x1, local copies, waits for them, and re-layouts: none -> 0.66 us  [by_realizations(): return (received[0].astype(f32), received[1].astype(f32))]
    squeeze x1 -> x0, local copies, waits for them, and re-layouts: 0.66 us -> none  [by_realizations(): return (received[0], received[1])]
where the time goes in v3:
time: 58.4 us; the launch traced here: 58 us
  Pallas kernels  30.2 us (52%)
  blocking collectives  9.62 us (16%)
  waiting for transfers between devices  8.97 us (15%)
  starting transfers between devices  7.82 us (13%)
  local copies, waits for them, and re-layouts  0.71 us (1%)
  between operations  0.71 us (1%)
    pallas_call x1, Pallas kernels, by_realizations(): pl.pallas_call(functools.partial(first_kernel, plan), out_shape=(pltpu.VM...  14.8 us
    all_to_all x1, blocking collectives, by_realizations(): received = lax.all_to_all(result, axes, 0, 0, tiled=True)  9.62 us
    pallas_call x2, Pallas kernels, by_realizations(): pl.pallas_call(functools.partial(next_kernel, first), out_shape=(field_sh...  7.61 us
    all_to_all x1, starting transfers between devices, by_realizations(): lax.all_to_all(outgoing, axes, 0, 0, tiled=True).reshape(blocks, 8, BLOCK)  7.3 us
    pallas_call x1, Pallas kernels, by_realizations(): pl.pallas_call(functools.partial(listing_kernel, plan, blocks), out_shape...  5.9 us
    all_to_all x1, waiting for transfers between devices, by_realizations(): lax.all_to_all(outgoing, axes, 0, 0, tiled=True).reshape(blocks, 8, BLOCK)  4.69 us
    ppermute x3, waiting for transfers between devices, by_realizations(): other = lax.ppermute(mine, 'col', swap)  4.28 us
    pallas_call x1, Pallas kernels, by_realizations(): pl.pallas_call(packing_kernel, out_shape=jax.ShapeDtypeStruct((devices, b...  1.6 us
  transfers between devices with their start and end apart: 4, of which 4 were waited for; matrix products, arithmetic and copies ran while one was open for 0% of the time, Pallas kernels for 10%

profile of v3, /device:TPU:0, one launch (start us, length us, event | category | flops | bytes accessed | tf_op | source)
XLA Modules:
  0.0 58.0 jit_solution(1422708567995112308)
XLA Ops:
  0.6 1.6 %shard_map.50 = f32[32,2,8,128]{3,2,1,0:T(8,128)} custom-call(f32[4,256]{1,0:T(4,128)} %point_hbm.1, f32[64,256]{1,0:T(8,128)} %field_hbm.1), custom_call_target="tpu_custom_call" | custom-call | tf_op jit(solution)/shard_map/pallas_call | solution.py:491
  2.2 7.3 %all-to-all-start = ((f32[32,2,8,128]{3,2,1,0:T(8,128)}), f32[32,2,8,128]{3,2,1,0:T(8,128)S(1)}, u32[]{:S(2)}, u32[]{:S(2)}) async-start(f32[32,2,8,128]{3,2,1,0:T(8,128)} %shard_map.50), calls=%async_computation | async-start | bytes 524288 | tf_op jit(solution)/shard_map/all_to_all | solution.py:521
  9.6 5.9 %shard_map.51 = (s32[232]{0:T(256)S(4)}, s32[904]{0:T(1024)S(4)}, s32[1]{0:T(128)S(4)}, s32[266]{0:T(512)S(4)}, s32[266]{0:T(512)S(4)}) custom-call(s32[1]{0:T(128)} %bitcast.core_ref, s32[2,468]{1,0:T(2,128)} %pair_ref.1), custom_call_target="tpu_custom_call" | custom-call | flops 8000000000 | bytes 20000000 | tf_op jit(solution)/shard_map/pallas_call | solution.py:506
  15.5 4.7 %all-to-all-done = f32[32,2,8,128]{3,2,1,0:T(8,128)S(1)} async-done(((f32[32,2,8,128]{3,2,1,0:T(8,128)}), f32[32,2,8,128]{3,2,1,0:T(8,128)S(1)}, u32[]{:S(2)}, u32[]{:S(2)}) %all-to-all-start) | async-done | bytes 262176 | tf_op jit(solution)/shard_map/all_to_all | solution.py:521
  20.1 14.8 %shard_map.52 = (bf16[532,128,128]{2,1,0:T(8,128)(2,1)S(1)}, f32[64,8,128]{2,1,0:T(8,128)S(1)}) custom-call(s32[266]{0:T(512)S(4)} %get-tuple-element.16.low_ref, s32[266]{0:T(512)S(4)} %get-tuple-element.17.high_ref, f32[64,8,128]{2,1,0:T(8,128)S(1)} %bitcast.15), custom_call_target="tpu_custom_call" | custom-call | tf_op jit(solution)/shard_map/pallas_call | solution.py:527
  34.9 0.1 collective-permute-start
  35.0 1.5 %collective-permute-done.other_ref = f32[64,8,128]{2,1,0:T(8,128)S(1)} collective-permute-done((f32[64,8,128]{2,1,0:T(8,128)S(1)}, f32[64,8,128]{2,1,0:T(8,128)S(1)}, u32[]{:S(2)}, u32[]{:S(2)}) %collective-permute-start) | collective-permute-done | bytes 262176 | tf_op jit(solution)/shard_map/ppermute | solution.py:544
  36.5 3.8 %shard_map.53 = (f32[64,8,128]{2,1,0:T(8,128)S(1)}, f32[3,64,8,128]{3,2,1,0:T(8,128)S(1)}) custom-call(s32[232]{0:T(256)S(4)} %get-tuple-element.13.owner_ref, s32[904]{0:T(1024)S(4)} %get-tuple-element.14.entry_ref, s32[1]{0:T(128)S(4)} %get-tuple-element.15.count_ref, f32[64,8,128]{2,1,0:T(8,128)S(1)} %bitcast.16, ...), custom_call_target="tpu_custom_call" | custom-call | tf_op jit(solution)/shard_map/pallas_call | solution.py:547
  40.3 0.2 collective-permute-start.1
  40.5 1.4 %collective-permute-done.1.other_ref = f32[64,8,128]{2,1,0:T(8,128)S(1)} collective-permute-done((f32[64,8,128]{2,1,0:T(8,128)S(1)}, f32[64,8,128]{2,1,0:T(8,128)S(1)}, u32[]{:S(2)}, u32[]{:S(2)}) %collective-permute-start.1) | collective-permute-done | bytes 262176 | tf_op jit(solution)/shard_map/ppermute | solution.py:544
  41.9 3.8 %shard_map.54 = (f32[64,8,128]{2,1,0:T(8,128)S(1)}, f32[3,64,8,128]{3,2,1,0:T(8,128)S(1)}) custom-call(s32[232]{0:T(256)S(4)} %get-tuple-element.13.owner_ref, s32[904]{0:T(1024)S(4)} %get-tuple-element.14.entry_ref, s32[1]{0:T(128)S(4)} %get-tuple-element.15.count_ref, f32[64,8,128]{2,1,0:T(8,128)S(1)} %bitcast.17, ...), custom_call_target="tpu_custom_call" | custom-call | tf_op jit(solution)/shard_map/pallas_call | solution.py:547
  45.7 0.2 collective-permute-start.2
  46.0 1.4 %collective-permute-done.2.other_ref = f32[64,8,128]{2,1,0:T(8,128)S(1)} collective-permute-done((f32[64,8,128]{2,1,0:T(8,128)S(1)}, f32[64,8,128]{2,1,0:T(8,128)S(1)}, u32[]{:S(2)}, u32[]{:S(2)}) %collective-permute-start.2) | collective-permute-done | bytes 262176 | tf_op jit(solution)/shard_map/ppermute | solution.py:555
  47.3 0.3 shard_map.55
  47.6 9.6 %all_to_all.10 = bf16[32,2,4,128]{3,2,1,0:T(4,128)(2,1)S(1)} all-to-all(bf16[32,2,4,128]{3,2,1,0:T(4,128)(2,1)S(1)} %bitcast.19), channel_id=1, replica_groups=mesh['row'=4,'col'=8] {'row','col'}, dimensions={0} | all-to-all | bytes 131072 | tf_op jit(solution)/shard_map/all_to_all | solution.py:564
  57.3 0.1 copy.11
  57.4 0.7 %copy_bitcast_fusion = (f32[64,256]{1,0:T(8,128)}, f32[64,256]{1,0:T(8,128)}) fusion(f32[8,8,2,128]{3,2,1,0:T(2,128)S(1)} %bitcast.21, f32[8,8,2,128]{3,2,1,0:T(2,128)S(1)} %bitcast.22), kind=kLoop, calls=%fused_computation | loop fusion | bytes 262144 | tf_op jit(solution)/shard_map/convert_element_type | solution.py:567
  (1 shorter events, 0.0 us)
Async XLA Ops:
  2.2 17.9 %all-to-all-start = ((f32[32,2,8,128]{3,2,1,0:T(8,128)}), f32[32,2,8,128]{3,2,1,0:T(8,128)S(1)}, u32[]{:S(2)}, u32[]{:S(2)}) async-start(f32[32,2,8,128]{3,2,1,0:T(8,128)} %shard_map.50), calls=%async_computation | async-start | bytes 524288 | tf_op jit(solution)/shard_map/all_to_all | solution.py:521
  34.9 1.6 %collective-permute-start = (f32[64,8,128]{2,1,0:T(8,128)S(1)}, f32[64,8,128]{2,1,0:T(8,128)S(1)}, u32[]{:S(2)}, u32[]{:S(2)}) collective-permute-start(f32[64,8,128]{2,1,0:T(8,128)S(1)} %get-tuple-element.18.mine_ref), channel_id=1, source_target_pairs={{0,1},{1,0},{2,3},{3,2},{4,5},{5,4},{6,7},{7,6},{8,9},{9,8},{10,11... | collective-permute-start | bytes 786440 | tf_op jit(solution)/shard_map/ppermute | solution.py:544
  40.3 1.6 %collective-permute-start.1 = (f32[64,8,128]{2,1,0:T(8,128)S(1)}, f32[64,8,128]{2,1,0:T(8,128)S(1)}, u32[]{:S(2)}, u32[]{:S(2)}) collective-permute-start(f32[64,8,128]{2,1,0:T(8,128)S(1)} %get-tuple-element.20.mine_ref), channel_id=1, source_target_pairs={{0,1},{1,0},{2,3},{3,2},{4,5},{5,4},{6,7},{7,6},{8,9},{9,8},{10,11... | collective-permute-start | bytes 786440 | tf_op jit(solution)/shard_map/ppermute | solution.py:544
  45.7 1.6 %collective-permute-start.2 = (f32[64,8,128]{2,1,0:T(8,128)S(1)}, f32[64,8,128]{2,1,0:T(8,128)S(1)}, u32[]{:S(2)}, u32[]{:S(2)}) collective-permute-start(f32[64,8,128]{2,1,0:T(8,128)S(1)} %get-tuple-element.22.mine_ref), channel_id=1, source_target_pairs={{0,1},{1,0},{2,3},{3,2},{4,5},{5,4},{6,7},{7,6},{8,9},{9,8},{10,11... | collective-permute-start | bytes 786440 | tf_op jit(solution)/shard_map/ppermute | solution.py:555

commit v4 on v3

--- a/solution.py
+++ b/solution.py
@@ -174,7 +174,7 @@
 
 
 def packing_kernel(point_hbm, field_hbm, outgoing_ref, point_ref, field_ref, arrived):
-    devices, blocks_here = outgoing_ref.shape[0:2]
+    devices = outgoing_ref.shape[0]
     copies = (
         pltpu.make_async_copy(point_hbm, point_ref, arrived.at[0]),
         pltpu.make_async_copy(field_hbm, field_ref, arrived.at[1]),
@@ -183,27 +183,41 @@
         copy.start()
     for copy in copies:
         copy.wait()
+    first = point_ref[:, 0:BLOCK]
+    second = point_ref[:, BLOCK : 2 * BLOCK]
+    first_high = first.astype(bf16).astype(f32)
+    second_high = second.astype(bf16).astype(f32)
     for chip in range(devices // 2):
-        for block in range(blocks_here):
-            place = pl.ds(block * BLOCK, BLOCK)
-            fields = field_ref[pl.ds(chip * rows_here, rows_here), place]
-            both = jnp.concatenate([fields, point_ref[:, place]], axis=0)
-            outgoing_ref[2 * chip, block] = both
-            outgoing_ref[2 * chip + 1, block] = both
+        rows = pl.ds(chip * rows_here, rows_here)
+        parts = (
+            field_ref[rows, 0:BLOCK],
+            first_high,
+            field_ref[rows, BLOCK : 2 * BLOCK],
+            second_high,
+            second - second_high,
+            first - first_high,
+        )
+        message = jnp.concatenate(parts, axis=0).astype(bf16)
+        outgoing_ref[2 * chip] = message
+        outgoing_ref[2 * chip + 1] = message
 
 
 def listing_kernel(
     plan,
     blocks,
     core_ref,
-    pair_ref,
+    pair_hbm,
     owner_ref,
     entry_ref,
     count_ref,
     low_ref,
     high_ref,
     open_ref,
+    pair_ref,
+    arrived,
 ):
+    copy = pltpu.make_async_copy(pair_hbm, pair_ref, arrived)
+    copy.start()
     half, width, steps, chunks = plan
     listed = pair_ref.shape[1]
     core = core_ref[0]
@@ -248,7 +262,8 @@
     for number in range(half + blocks // 2, slots):
         low_ref[number] = blocks
         high_ref[number] = blocks
-    used = lax.fori_loop(0, listed // 2, list_pair, 0, unroll=8)
+    copy.wait()
+    used = lax.fori_loop(0, listed // 2, list_pair, 0, unroll=13)
     if listed % 2:
         used = lax.fori_loop(half - 1, half - core, list_pair, used)
     used = lax.fori_loop(0, blocks // 2, list_diagonal, used, unroll=8)
@@ -264,7 +279,8 @@
     near = jnp.maximum(1.0 - distance * (1.0 / long_range), 0.0)
     near_square = near * near
     wide = near_square * near_square * (1.25 - near)
-    close = jnp.maximum(1.0 - distance * (1.0 / short_range), 0.0).astype(bf16)
+    close = (1.0 - distance * (1.0 / short_range)).astype(bf16)
+    close = jnp.maximum(close, jnp.asarray(0.0, bf16))
     close_square = close * close
     narrow = close_square * close_square * (jnp.asarray(1.25, bf16) - close)
     return wide.astype(bf16) + narrow
@@ -282,10 +298,10 @@
 
 
 def store_scaled(fields_ref, direction, scale):
-    scaled = jnp.where(row_number(direction.shape) < rows_here, direction * (4.0 * scale), 0.0)
     blocks = direction.shape[0]
-    doubled = jnp.concatenate([scaled, jnp.zeros_like(scaled)], axis=1)
-    fields_ref[0:blocks] = doubled.astype(bf16)
+    blank = jnp.zeros((blocks, 16 - rows_here, BLOCK), f32)
+    scaled = jnp.concatenate([direction * (4.0 * scale), blank], axis=1)
+    fields_ref[0:blocks] = scaled.astype(bf16)
     fields_ref[blocks] = jnp.zeros((16, BLOCK), bf16)
 
 
@@ -318,9 +334,10 @@
     plan,
     low_ref,
     high_ref,
-    gathered_ref,
+    received_ref,
     tiles_ref,
     product_ref,
+    gathered_ref,
     left_ref,
     right_ref,
     fields_ref,
@@ -330,6 +347,14 @@
     half, width, steps, _ = plan
     blocks = gathered_ref.shape[0]
     slots = width * steps
+    for device in range(blocks // 2):
+        message = received_ref[device].astype(f32)
+        lower = message[16:24]
+        is_point = row_number((8, BLOCK)) >= rows_here
+        first = message[0:8] + jnp.where(is_point, lower, 0.0)
+        second = message[8:16] + jnp.where(is_point, pltpu.roll(lower, 4, axis=0), 0.0)
+        gathered_ref[2 * device] = first
+        gathered_ref[2 * device + 1] = second
     highest = jnp.max(jnp.max(gathered_ref[...], axis=0), axis=1, keepdims=True)
     lowest = jnp.min(jnp.min(gathered_ref[...], axis=0), axis=1, keepdims=True)
     centre = 0.5 * (highest + lowest)
@@ -352,7 +377,7 @@
     lax.fori_loop(0, blocks, prepare, 0, unroll=8)
     left_ref[blocks] = jnp.zeros((BLOCK, 48), bf16)
     right_ref[blocks] = jnp.zeros((48, BLOCK), bf16)
-    store_scaled(fields_ref, gathered_ref[...], gathered_ref[:, 7:8, :])
+    store_scaled(fields_ref, gathered_ref[:, 0:rows_here, :], gathered_ref[:, 7:8, :])
     totals_ref[...] = jnp.zeros_like(totals_ref)
 
     def square(step, slot):
@@ -417,7 +442,7 @@
 
     lax.fori_loop(0, steps // 2, both_steps, 0)
     use_tiles(steps - 1, odd)
-    product_ref[...] = totals_ref[0:blocks]
+    product_ref[...] = totals_ref[0:blocks, 0:rows_here, :]
 
 
 def total(values):
@@ -425,11 +450,10 @@
 
 
 def advance(mine_ref, other_ref, scale, direction, residual):
-    row = row_number((1, 8, 1))
     image = nugget * direction + scale * (mine_ref[...] + other_ref[...])
     norm_now = total(residual * residual)
     along = total(direction * image)
-    alpha = norm_now / jnp.where(row < rows_here, along, 1.0)
+    alpha = norm_now / along
     return alpha * direction, residual - alpha * image, norm_now
 
 
@@ -445,8 +469,7 @@
 ):
     if first:
         tiles_ref, product_ref, state_out_ref, fields_ref, totals_ref = rest
-        row = row_number(gathered_ref.shape)
-        direction = jnp.where(row < rows_here, gathered_ref[...], 0.0)
+        direction = gathered_ref[:, 0:rows_here, :]
         residual = direction
     else:
         state_ref, tiles_ref, product_ref, state_out_ref, fields_ref, totals_ref = rest
@@ -455,22 +478,20 @@
     scale = gathered_ref[:, 7:8, :]
     moved, residual, norm_now = advance(mine_ref, other_ref, scale, direction, residual)
     norm_next = total(residual * residual)
-    row = row_number((1, 8, 1))
-    beta = norm_next / jnp.where(row < rows_here, norm_now, 1.0)
-    direction = residual + beta * direction
+    direction = residual + (norm_next / norm_now) * direction
     state_out_ref[0] = moved if first else state_ref[0] + moved
     state_out_ref[1] = residual
     state_out_ref[2] = direction
     store_scaled(fields_ref, direction, scale)
     multiply(owner_ref, entry_ref, count_ref[0], tiles_ref, fields_ref, totals_ref)
-    product_ref[...] = totals_ref[0 : gathered_ref.shape[0]]
+    product_ref[...] = totals_ref[0 : gathered_ref.shape[0], 0:rows_here, :]
 
 
 def last_kernel(core_ref, gathered_ref, mine_ref, other_ref, state_ref, result_ref):
     scale = gathered_ref[:, 7:8, :]
     moved, residual, _ = advance(mine_ref, other_ref, scale, state_ref[2], state_ref[1])
     chosen = jnp.where(core_ref[0] == 0, state_ref[0] + moved, residual)
-    result_ref[...] = chosen[:, 0:rows_here, :].astype(bf16)
+    result_ref[...] = chosen.astype(bf16)
 
 
 def by_realizations(point_data, right_side, pair_list):
@@ -490,7 +511,7 @@
     limits = pltpu.CompilerParams(vmem_limit_bytes=kernel_bytes)
     outgoing = pl.pallas_call(
         packing_kernel,
-        out_shape=jax.ShapeDtypeStruct((devices, blocks_here, 8, BLOCK), f32),
+        out_shape=jax.ShapeDtypeStruct((devices, 24, BLOCK), bf16),
         in_specs=[pl.BlockSpec(memory_space=pltpu.HBM)] * 2,
         out_specs=vector,
         scratch_shapes=[
@@ -512,23 +533,28 @@
             pltpu.SMEM((slots,), jnp.int32),
             pltpu.SMEM((slots,), jnp.int32),
         ),
-        in_specs=[scalar, scalar],
+        in_specs=[scalar, pl.BlockSpec(memory_space=pltpu.HBM)],
         out_specs=(scalar,) * 5,
-        scratch_shapes=[pltpu.SMEM((blocks,), jnp.int32)],
+        scratch_shapes=[
+            pltpu.SMEM((blocks,), jnp.int32),
+            pltpu.SMEM(pair_list.shape, jnp.int32),
+            pltpu.SemaphoreType.DMA,
+        ],
         cost_estimate=pl.CostEstimate(flops=8_000_000_000, bytes_accessed=20_000_000, transcendentals=0),
         compiler_params=limits,
     )(core, pltpu.with_memory_space_constraint(pair_list, pltpu.HBM))
-    gathered = lax.all_to_all(outgoing, axes, 0, 0, tiled=True).reshape(blocks, 8, BLOCK)
+    received = lax.all_to_all(outgoing, axes, 0, 0, tiled=True)
 
     field_shape = jax.ShapeDtypeStruct((blocks, 8, BLOCK), f32)
-    state_shape = jax.ShapeDtypeStruct((3, blocks, 8, BLOCK), f32)
+    product_shape = jax.ShapeDtypeStruct((blocks, rows_here, BLOCK), f32)
+    state_shape = jax.ShapeDtypeStruct((3, blocks, rows_here, BLOCK), f32)
     work = [pltpu.VMEM((blocks + 1, 16, BLOCK), bf16), pltpu.VMEM((blocks + 1, 8, BLOCK), f32)]
     stage = pltpu.VMEM((width, BLOCK, BLOCK), bf16)
-    tiles, mine = pl.pallas_call(
+    tiles, mine, gathered = pl.pallas_call(
         functools.partial(first_kernel, plan),
-        out_shape=(pltpu.VMEM((2 * slots, BLOCK, BLOCK), bf16), field_shape),
+        out_shape=(pltpu.VMEM((2 * slots, BLOCK, BLOCK), bf16), product_shape, field_shape),
         in_specs=[scalar, scalar, vector],
-        out_specs=(vector, vector),
+        out_specs=(vector, vector, vector),
         scratch_shapes=[
             pltpu.VMEM((blocks + 1, BLOCK, 48), bf16),
             pltpu.VMEM((blocks + 1, 48, BLOCK), bf16),
@@ -536,7 +562,7 @@
             *[stage] * 4,
         ],
         compiler_params=limits,
-    )(low, high, gathered)
+    )(low, high, received)
     tiles = pltpu.with_memory_space_constraint(tiles, pltpu.VMEM)
     swap = [(place, place ^ 1) for place in range(col_devices)]
     state = None
@@ -546,7 +572,7 @@
         carried = () if first else (state,)
         mine, state = pl.pallas_call(
             functools.partial(next_kernel, first),
-            out_shape=(field_shape, state_shape),
+            out_shape=(product_shape, state_shape),
             in_specs=[scalar, scalar, scalar] + [vector] * (4 + len(carried)),
             out_specs=(vector, vector),
             scratch_shapes=work,
@@ -573,7 +599,7 @@
     blocks = point_data.shape[1] // BLOCK * devices
     _, width, steps, _ = tile_schedule(pair_list.shape[1], blocks)
     tile_bytes = 2 * width * steps * BLOCK * BLOCK * 2
-    paired = col_devices % 2 == 0 and blocks % 2 == 0
+    paired = col_devices % 2 == 0 and blocks == 2 * devices
     if paired and right_side.shape[0] == rows_here * (devices // 2) and tile_bytes <= tile_bytes_limit:
         return by_realizations(point_data, right_side, pair_list)
     return by_points(point_data, right_side, pair_list)

time: 58.4 us -> 56.1 us (0.961)
  waiting for transfers between devices: 8.97 us -> 6.68 us
  starting transfers between devices: 7.82 us -> 8.83 us
  Pallas kernels: 30.2 us -> 29.2 us
    ppermute x3, waiting for transfers between devices: 4.28 us -> 2.96 us  [by_realizations(): other = lax.ppermute(mine, 'col', swap)]
    ppermute x3, starting transfers between devices: 0.51 us -> 1.53 us  [by_realizations(): other = lax.ppermute(mine, 'col', swap)]
    all_to_all x1, waiting for transfers between devices: 4.69 us -> 3.72 us  [by_realizations(): received = lax.all_to_all(outgoing, axes, 0, 0, tiled=True)]
    pallas_call x1, Pallas kernels: 5.9 us -> 5.16 us  [by_realizations(): pl.pallas_call(functools.partial(listing_kernel, plan, blocks), out_shape...]
  transfers between devices with their start and end apart: 4 -> 4, of which waited for: 4 -> 4; matrix products, arithmetic and copies ran while one was open for 0% -> 0% of each run, Pallas kernels for 10% -> 9%
where the time goes in v4:
time: 56.1 us; the launch traced here: 55.9 us
  Pallas kernels  29.2 us (52%)
  blocking collectives  9.68 us (17%)
  starting transfers between devices  8.83 us (16%)
  waiting for transfers between devices  6.68 us (12%)
  local copies, waits for them, and re-layouts  0.71 us (1%)
  between operations  0.7 us (1%)
    pallas_call x1, Pallas kernels, by_realizations(): pl.pallas_call(functools.partial(first_kernel, plan), out_shape=(pltpu.VM...  14.5 us
    all_to_all x1, blocking collectives, by_realizations(): received = lax.all_to_all(result, axes, 0, 0, tiled=True)  9.68 us
    pallas_call x2, Pallas kernels, by_realizations(): pl.pallas_call(functools.partial(next_kernel, first), out_shape=(product_...  7.66 us
    all_to_all x1, starting transfers between devices, by_realizations(): received = lax.all_to_all(outgoing, axes, 0, 0, tiled=True)  7.3 us
    pallas_call x1, Pallas kernels, by_realizations(): pl.pallas_call(functools.partial(listing_kernel, plan, blocks), out_shape...  5.16 us
    all_to_all x1, waiting for transfers between devices, by_realizations(): received = lax.all_to_all(outgoing, axes, 0, 0, tiled=True)  3.72 us
    ppermute x3, waiting for transfers between devices, by_realizations(): other = lax.ppermute(mine, 'col', swap)  2.96 us
    pallas_call x1, Pallas kernels, by_realizations(): pl.pallas_call(packing_kernel, out_shape=jax.ShapeDtypeStruct((devices, 2...  1.57 us
  transfers between devices with their start and end apart: 4, of which 4 were waited for; matrix products, arithmetic and copies ran while one was open for 0% of the time, Pallas kernels for 9%

profile of v4, /device:TPU:0, one launch (start us, length us, event | category | flops | bytes accessed | tf_op | source)
XLA Modules:
  0.0 55.9 jit_solution(15244198725339861209)
XLA Ops:
  0.6 1.6 %shard_map.51 = bf16[32,24,128]{2,1,0:T(8,128)(2,1)} custom-call(f32[4,256]{1,0:T(4,128)} %point_hbm.1, f32[64,256]{1,0:T(8,128)} %field_hbm.1), custom_call_target="tpu_custom_call" | custom-call | tf_op jit(solution)/shard_map/pallas_call | solution.py:512
  2.2 7.3 %all-to-all-start = ((bf16[32,24,128]{2,1,0:T(8,128)(2,1)}), bf16[32,24,128]{2,1,0:T(8,128)(2,1)S(1)}, u32[]{:S(2)}, u32[]{:S(2)}) async-start(bf16[32,24,128]{2,1,0:T(8,128)(2,1)} %shard_map.51), calls=%async_computation | async-start | bytes 393216 | tf_op jit(solution)/shard_map/all_to_all | solution.py:546
  9.5 5.2 %shard_map.50 = (s32[232]{0:T(256)S(4)}, s32[904]{0:T(1024)S(4)}, s32[1]{0:T(128)S(4)}, s32[266]{0:T(512)S(4)}, s32[266]{0:T(512)S(4)}) custom-call(s32[1]{0:T(128)} %bitcast.core_ref, s32[2,468]{1,0:T(2,128)} %pair_hbm.1), custom_call_target="tpu_custom_call" | custom-call | flops 8000000000 | bytes 20000000 | tf_op jit(solution)/shard_map/pallas_call | solution.py:527
  14.7 3.7 %all-to-all-done.received_ref = bf16[32,24,128]{2,1,0:T(8,128)(2,1)S(1)} async-done(((bf16[32,24,128]{2,1,0:T(8,128)(2,1)}), bf16[32,24,128]{2,1,0:T(8,128)(2,1)S(1)}, u32[]{:S(2)}, u32[]{:S(2)}) %all-to-all-start) | async-done | bytes 196640 | tf_op jit(solution)/shard_map/all_to_all | solution.py:546
  18.4 14.5 %shard_map.52 = (bf16[532,128,128]{2,1,0:T(8,128)(2,1)S(1)}, f32[64,4,128]{2,1,0:T(4,128)S(1)}, f32[64,8,128]{2,1,0:T(8,128)S(1)}) custom-call(s32[266]{0:T(512)S(4)} %get-tuple-element.14.low_ref, s32[266]{0:T(512)S(4)} %get-tuple-element.15.high_ref, bf16[32,24,128]{2,1,0:T(8,128)(2,1)S(1)} %all-to-all-done.received_ref), custom_call_target="tpu_custom_call" | custom-call | tf_op jit(solution)/shard_map/pallas_call | solution.py:553
  32.9 0.7 %collective-permute-start = (f32[64,4,128]{2,1,0:T(4,128)S(1)}, f32[64,4,128]{2,1,0:T(4,128)S(1)}, u32[]{:S(2)}, u32[]{:S(2)}) collective-permute-start(f32[64,4,128]{2,1,0:T(4,128)S(1)} %get-tuple-element.20.mine_ref), channel_id=1, source_target_pairs={{0,1},{1,0},{2,3},{3,2},{4,5},{5,4},{6,7},{7,6},{8,9},{9,8},{10,11... | collective-permute-start | bytes 393224 | tf_op jit(solution)/shard_map/ppermute | solution.py:570
  33.6 1.0 %collective-permute-done.other_ref = f32[64,4,128]{2,1,0:T(4,128)S(1)} collective-permute-done((f32[64,4,128]{2,1,0:T(4,128)S(1)}, f32[64,4,128]{2,1,0:T(4,128)S(1)}, u32[]{:S(2)}, u32[]{:S(2)}) %collective-permute-start) | collective-permute-done | bytes 131104 | tf_op jit(solution)/shard_map/ppermute | solution.py:570
  34.6 3.8 %shard_map.53 = (f32[64,4,128]{2,1,0:T(4,128)S(1)}, f32[3,64,4,128]{3,2,1,0:T(4,128)S(1)}) custom-call(s32[232]{0:T(256)S(4)} %get-tuple-element.17.owner_ref, s32[904]{0:T(1024)S(4)} %get-tuple-element.18.entry_ref, s32[1]{0:T(128)S(4)} %get-tuple-element.19.count_ref, f32[64,8,128]{2,1,0:T(8,128)S(1)} %get-tuple-element.16.gathered_ref, ...), custom_call_target="tpu_custom_call" | custom-call | tf_op jit(solution)/shard_map/pallas_call | solution.py:573
  38.4 0.4 collective-permute-start.1
  38.9 1.0 %collective-permute-done.1.other_ref = f32[64,4,128]{2,1,0:T(4,128)S(1)} collective-permute-done((f32[64,4,128]{2,1,0:T(4,128)S(1)}, f32[64,4,128]{2,1,0:T(4,128)S(1)}, u32[]{:S(2)}, u32[]{:S(2)}) %collective-permute-start.1) | collective-permute-done | bytes 131104 | tf_op jit(solution)/shard_map/ppermute | solution.py:570
  39.9 3.8 %shard_map.54 = (f32[64,4,128]{2,1,0:T(4,128)S(1)}, f32[3,64,4,128]{3,2,1,0:T(4,128)S(1)}) custom-call(s32[232]{0:T(256)S(4)} %get-tuple-element.17.owner_ref, s32[904]{0:T(1024)S(4)} %get-tuple-element.18.entry_ref, s32[1]{0:T(128)S(4)} %get-tuple-element.19.count_ref, f32[64,8,128]{2,1,0:T(8,128)S(1)} %get-tuple-element.16.gathered_ref, ...), custom_call_target="tpu_custom_call" | custom-call | tf_op jit(solution)/shard_map/pallas_call | solution.py:573
  43.7 0.4 collective-permute-start.2
  44.1 1.0 %collective-permute-done.2.other_ref = f32[64,4,128]{2,1,0:T(4,128)S(1)} collective-permute-done((f32[64,4,128]{2,1,0:T(4,128)S(1)}, f32[64,4,128]{2,1,0:T(4,128)S(1)}, u32[]{:S(2)}, u32[]{:S(2)}) %collective-permute-start.2) | collective-permute-done | bytes 131104 | tf_op jit(solution)/shard_map/ppermute | solution.py:581
  45.1 0.3 shard_map.55
  45.4 9.7 %all_to_all.10 = bf16[32,2,4,128]{3,2,1,0:T(4,128)(2,1)S(1)} all-to-all(bf16[32,2,4,128]{3,2,1,0:T(4,128)(2,1)S(1)} %bitcast.14), channel_id=1, replica_groups=mesh['row'=4,'col'=8] {'row','col'}, dimensions={0} | all-to-all | bytes 131072 | tf_op jit(solution)/shard_map/all_to_all | solution.py:590
  55.1 0.1 copy.11
  55.2 0.7 %copy_bitcast_fusion = (f32[64,256]{1,0:T(8,128)}, f32[64,256]{1,0:T(8,128)}) fusion(f32[8,8,2,128]{3,2,1,0:T(2,128)S(1)} %bitcast.16, f32[8,8,2,128]{3,2,1,0:T(2,128)S(1)} %bitcast.17), kind=kLoop, calls=%fused_computation | loop fusion | bytes 262144 | tf_op jit(solution)/shard_map/convert_element_type | solution.py:593
  (1 shorter events, 0.0 us)
Async XLA Ops:
  2.2 16.2 %all-to-all-start = ((bf16[32,24,128]{2,1,0:T(8,128)(2,1)}), bf16[32,24,128]{2,1,0:T(8,128)(2,1)S(1)}, u32[]{:S(2)}, u32[]{:S(2)}) async-start(bf16[32,24,128]{2,1,0:T(8,128)(2,1)} %shard_map.51), calls=%async_computation | async-start | bytes 393216 | tf_op jit(solution)/shard_map/all_to_all | solution.py:546
  32.9 1.7 %collective-permute-start = (f32[64,4,128]{2,1,0:T(4,128)S(1)}, f32[64,4,128]{2,1,0:T(4,128)S(1)}, u32[]{:S(2)}, u32[]{:S(2)}) collective-permute-start(f32[64,4,128]{2,1,0:T(4,128)S(1)} %get-tuple-element.20.mine_ref), channel_id=1, source_target_pairs={{0,1},{1,0},{2,3},{3,2},{4,5},{5,4},{6,7},{7,6},{8,9},{9,8},{10,11... | collective-permute-start | bytes 393224 | tf_op jit(solution)/shard_map/ppermute | solution.py:570
  38.4 1.4 %collective-permute-start.1 = (f32[64,4,128]{2,1,0:T(4,128)S(1)}, f32[64,4,128]{2,1,0:T(4,128)S(1)}, u32[]{:S(2)}, u32[]{:S(2)}) collective-permute-start(f32[64,4,128]{2,1,0:T(4,128)S(1)} %get-tuple-element.22.mine_ref), channel_id=1, source_target_pairs={{0,1},{1,0},{2,3},{3,2},{4,5},{5,4},{6,7},{7,6},{8,9},{9,8},{10,11... | collective-permute-start | bytes 393224 | tf_op jit(solution)/shard_map/ppermute | solution.py:570
  43.7 1.4 %collective-permute-start.2 = (f32[64,4,128]{2,1,0:T(4,128)S(1)}, f32[64,4,128]{2,1,0:T(4,128)S(1)}, u32[]{:S(2)}, u32[]{:S(2)}) collective-permute-start(f32[64,4,128]{2,1,0:T(4,128)S(1)} %get-tuple-element.24.mine_ref), channel_id=1, source_target_pairs={{0,1},{1,0},{2,3},{3,2},{4,5},{5,4},{6,7},{7,6},{8,9},{9,8},{10,11... | collective-permute-start | bytes 393224 | tf_op jit(solution)/shard_map/ppermute | solution.py:581

commit v5 on v4

--- a/solution.py
+++ b/solution.py
@@ -17,7 +17,7 @@
 rows_here = 4
 chunk_bits = 2
 chunk = 1 << chunk_bits
-chunks_per_step = 32
+chunks_per_step = 40
 tile_bytes_limit = 24 * 2**20
 kernel_bytes = 12 * 2**20
 f32 = jnp.float32
@@ -165,7 +165,7 @@
 def tile_schedule(listed, blocks):
     half = (listed + 1) // 2
     entries = half + blocks // 2
-    sizes = range(12, 21)
+    sizes = range(20, 39)
     width = min(sizes, key=lambda size: (-(-entries // (2 * size)) * size, -size))
     steps = -(-entries // (2 * width)) * 2
     longest = (2 * half + blocks // 2 + 3 * blocks) // chunk
@@ -279,7 +279,7 @@
     near = jnp.maximum(1.0 - distance * (1.0 / long_range), 0.0)
     near_square = near * near
     wide = near_square * near_square * (1.25 - near)
-    close = (1.0 - distance * (1.0 / short_range)).astype(bf16)
+    close = jnp.asarray(1.0, bf16) - distance.astype(bf16) * jnp.asarray(1.0 / short_range, bf16)
     close = jnp.maximum(close, jnp.asarray(0.0, bf16))
     close_square = close * close
     narrow = close_square * close_square * (jnp.asarray(1.25, bf16) - close)
@@ -374,7 +374,7 @@
         right_ref[block] = right_all.astype(bf16)
         return carry
 
-    lax.fori_loop(0, blocks, prepare, 0, unroll=8)
+    lax.fori_loop(0, blocks, prepare, 0, unroll=32)
     left_ref[blocks] = jnp.zeros((BLOCK, 48), bf16)
     right_ref[blocks] = jnp.zeros((48, BLOCK), bf16)
     store_scaled(fields_ref, gathered_ref[:, 0:rows_here, :], gathered_ref[:, 7:8, :])

time: 56.1 us -> 54.5 us (0.971)
  Pallas kernels: 29.2 us -> 27.7 us
    pallas_call x1, Pallas kernels: 14.5 us -> 13.2 us  [by_realizations(): pl.pallas_call(functools.partial(first_kernel, plan), out_shape=(pltpu.VM...]
  transfers between devices with their start and end apart: 4 -> 4, of which waited for: 4 -> 4; matrix products, arithmetic and copies ran while one was open for 0% -> 0% of each run, Pallas kernels for 9% -> 10%
where the time goes in v5:
time: 54.5 us; the launch traced here: 54.3 us
  Pallas kernels  27.7 us (51%)
  blocking collectives  9.72 us (18%)
  starting transfers between devices  8.79 us (16%)
  waiting for transfers between devices  6.61 us (12%)
  local copies, waits for them, and re-layouts  0.71 us (1%)
  between operations  0.7 us (1%)
    pallas_call x1, Pallas kernels, by_realizations(): pl.pallas_call(functools.partial(first_kernel, plan), out_shape=(pltpu.VM...  13.2 us
    all_to_all x1, blocking collectives, by_realizations(): received = lax.all_to_all(result, axes, 0, 0, tiled=True)  9.72 us
    pallas_call x2, Pallas kernels, by_realizations(): pl.pallas_call(functools.partial(next_kernel, first), out_shape=(product_...  7.43 us
    all_to_all x1, starting transfers between devices, by_realizations(): received = lax.all_to_all(outgoing, axes, 0, 0, tiled=True)  7.3 us
    pallas_call x1, Pallas kernels, by_realizations(): pl.pallas_call(functools.partial(listing_kernel, plan, blocks), out_shape...  5.22 us
    all_to_all x1, waiting for transfers between devices, by_realizations(): received = lax.all_to_all(outgoing, axes, 0, 0, tiled=True)  3.65 us
    ppermute x3, waiting for transfers between devices, by_realizations(): other = lax.ppermute(mine, 'col', swap)  2.96 us
    pallas_call x1, Pallas kernels, by_realizations(): pl.pallas_call(packing_kernel, out_shape=jax.ShapeDtypeStruct((devices, 2...  1.57 us
  transfers between devices with their start and end apart: 4, of which 4 were waited for; matrix products, arithmetic and copies ran while one was open for 0% of the time, Pallas kernels for 10%

profile of v5, /device:TPU:0, one launch (start us, length us, event | category | flops | bytes accessed | tf_op | source)
XLA Modules:
  0.0 54.3 jit_solution(10792239708831386433)
XLA Ops:
  0.6 1.6 %shard_map.51 = bf16[32,24,128]{2,1,0:T(8,128)(2,1)} custom-call(f32[4,256]{1,0:T(4,128)} %point_hbm.1, f32[64,256]{1,0:T(8,128)} %field_hbm.1), custom_call_target="tpu_custom_call" | custom-call | tf_op jit(solution)/shard_map/pallas_call | solution.py:512
  2.2 7.3 %all-to-all-start = ((bf16[32,24,128]{2,1,0:T(8,128)(2,1)}), bf16[32,24,128]{2,1,0:T(8,128)(2,1)S(1)}, u32[]{:S(2)}, u32[]{:S(2)}) async-start(bf16[32,24,128]{2,1,0:T(8,128)(2,1)} %shard_map.51), calls=%async_computation | async-start | bytes 393216 | tf_op jit(solution)/shard_map/all_to_all | solution.py:546
  9.5 5.2 %shard_map.50 = (s32[248]{0:T(256)S(4)}, s32[968]{0:T(1024)S(4)}, s32[1]{0:T(128)S(4)}, s32[270]{0:T(512)S(4)}, s32[270]{0:T(512)S(4)}) custom-call(s32[1]{0:T(128)} %bitcast.core_ref, s32[2,468]{1,0:T(2,128)} %pair_hbm.1), custom_call_target="tpu_custom_call" | custom-call | flops 8000000000 | bytes 20000000 | tf_op jit(solution)/shard_map/pallas_call | solution.py:527
  14.7 3.7 %all-to-all-done.received_ref = bf16[32,24,128]{2,1,0:T(8,128)(2,1)S(1)} async-done(((bf16[32,24,128]{2,1,0:T(8,128)(2,1)}), bf16[32,24,128]{2,1,0:T(8,128)(2,1)S(1)}, u32[]{:S(2)}, u32[]{:S(2)}) %all-to-all-start) | async-done | bytes 196640 | tf_op jit(solution)/shard_map/all_to_all | solution.py:546
  18.4 13.2 %shard_map.52 = (bf16[540,128,128]{2,1,0:T(8,128)(2,1)S(1)}, f32[64,4,128]{2,1,0:T(4,128)S(1)}, f32[64,8,128]{2,1,0:T(8,128)S(1)}) custom-call(s32[270]{0:T(512)S(4)} %get-tuple-element.14.low_ref, s32[270]{0:T(512)S(4)} %get-tuple-element.15.high_ref, bf16[32,24,128]{2,1,0:T(8,128)(2,1)S(1)} %all-to-all-done.received_ref), custom_call_target="tpu_custom_call" | custom-call | tf_op jit(solution)/shard_map/pallas_call | solution.py:553
  31.6 0.6 %collective-permute-start = (f32[64,4,128]{2,1,0:T(4,128)S(1)}, f32[64,4,128]{2,1,0:T(4,128)S(1)}, u32[]{:S(2)}, u32[]{:S(2)}) collective-permute-start(f32[64,4,128]{2,1,0:T(4,128)S(1)} %get-tuple-element.20.mine_ref), channel_id=1, source_target_pairs={{0,1},{1,0},{2,3},{3,2},{4,5},{5,4},{6,7},{7,6},{8,9},{9,8},{10,11... | collective-permute-start | bytes 393224 | tf_op jit(solution)/shard_map/ppermute | solution.py:570
  32.2 1.0 %collective-permute-done.other_ref = f32[64,4,128]{2,1,0:T(4,128)S(1)} collective-permute-done((f32[64,4,128]{2,1,0:T(4,128)S(1)}, f32[64,4,128]{2,1,0:T(4,128)S(1)}, u32[]{:S(2)}, u32[]{:S(2)}) %collective-permute-start) | collective-permute-done | bytes 131104 | tf_op jit(solution)/shard_map/ppermute | solution.py:570
  33.2 3.7 %shard_map.53 = (f32[64,4,128]{2,1,0:T(4,128)S(1)}, f32[3,64,4,128]{3,2,1,0:T(4,128)S(1)}) custom-call(s32[248]{0:T(256)S(4)} %get-tuple-element.17.owner_ref, s32[968]{0:T(1024)S(4)} %get-tuple-element.18.entry_ref, s32[1]{0:T(128)S(4)} %get-tuple-element.19.count_ref, f32[64,8,128]{2,1,0:T(8,128)S(1)} %get-tuple-element.16.gathered_ref, ...), custom_call_target="tpu_custom_call" | custom-call | tf_op jit(solution)/shard_map/pallas_call | solution.py:573
  36.9 0.4 collective-permute-start.1
  37.3 1.0 %collective-permute-done.1.other_ref = f32[64,4,128]{2,1,0:T(4,128)S(1)} collective-permute-done((f32[64,4,128]{2,1,0:T(4,128)S(1)}, f32[64,4,128]{2,1,0:T(4,128)S(1)}, u32[]{:S(2)}, u32[]{:S(2)}) %collective-permute-start.1) | collective-permute-done | bytes 131104 | tf_op jit(solution)/shard_map/ppermute | solution.py:570
  38.3 3.7 %shard_map.54 = (f32[64,4,128]{2,1,0:T(4,128)S(1)}, f32[3,64,4,128]{3,2,1,0:T(4,128)S(1)}) custom-call(s32[248]{0:T(256)S(4)} %get-tuple-element.17.owner_ref, s32[968]{0:T(1024)S(4)} %get-tuple-element.18.entry_ref, s32[1]{0:T(128)S(4)} %get-tuple-element.19.count_ref, f32[64,8,128]{2,1,0:T(8,128)S(1)} %get-tuple-element.16.gathered_ref, ...), custom_call_target="tpu_custom_call" | custom-call | tf_op jit(solution)/shard_map/pallas_call | solution.py:573
  42.0 0.4 collective-permute-start.2
  42.5 1.0 %collective-permute-done.2.other_ref = f32[64,4,128]{2,1,0:T(4,128)S(1)} collective-permute-done((f32[64,4,128]{2,1,0:T(4,128)S(1)}, f32[64,4,128]{2,1,0:T(4,128)S(1)}, u32[]{:S(2)}, u32[]{:S(2)}) %collective-permute-start.2) | collective-permute-done | bytes 131104 | tf_op jit(solution)/shard_map/ppermute | solution.py:581
  43.5 0.3 shard_map.55
  43.8 9.7 %all_to_all.10 = bf16[32,2,4,128]{3,2,1,0:T(4,128)(2,1)S(1)} all-to-all(bf16[32,2,4,128]{3,2,1,0:T(4,128)(2,1)S(1)} %bitcast.14), channel_id=1, replica_groups=mesh['row'=4,'col'=8] {'row','col'}, dimensions={0} | all-to-all | bytes 131072 | tf_op jit(solution)/shard_map/all_to_all | solution.py:590
  53.5 0.1 copy.11
  53.6 0.7 %copy_bitcast_fusion = (f32[64,256]{1,0:T(8,128)}, f32[64,256]{1,0:T(8,128)}) fusion(f32[8,8,2,128]{3,2,1,0:T(2,128)S(1)} %bitcast.16, f32[8,8,2,128]{3,2,1,0:T(2,128)S(1)} %bitcast.17), kind=kLoop, calls=%fused_computation | loop fusion | bytes 262144 | tf_op jit(solution)/shard_map/convert_element_type | solution.py:593
  (1 shorter events, 0.0 us)
Async XLA Ops:
  2.2 16.2 %all-to-all-start = ((bf16[32,24,128]{2,1,0:T(8,128)(2,1)}), bf16[32,24,128]{2,1,0:T(8,128)(2,1)S(1)}, u32[]{:S(2)}, u32[]{:S(2)}) async-start(bf16[32,24,128]{2,1,0:T(8,128)(2,1)} %shard_map.51), calls=%async_computation | async-start | bytes 393216 | tf_op jit(solution)/shard_map/all_to_all | solution.py:546
  31.6 1.6 %collective-permute-start = (f32[64,4,128]{2,1,0:T(4,128)S(1)}, f32[64,4,128]{2,1,0:T(4,128)S(1)}, u32[]{:S(2)}, u32[]{:S(2)}) collective-permute-start(f32[64,4,128]{2,1,0:T(4,128)S(1)} %get-tuple-element.20.mine_ref), channel_id=1, source_target_pairs={{0,1},{1,0},{2,3},{3,2},{4,5},{5,4},{6,7},{7,6},{8,9},{9,8},{10,11... | collective-permute-start | bytes 393224 | tf_op jit(solution)/shard_map/ppermute | solution.py:570
  36.9 1.4 %collective-permute-start.1 = (f32[64,4,128]{2,1,0:T(4,128)S(1)}, f32[64,4,128]{2,1,0:T(4,128)S(1)}, u32[]{:S(2)}, u32[]{:S(2)}) collective-permute-start(f32[64,4,128]{2,1,0:T(4,128)S(1)} %get-tuple-element.22.mine_ref), channel_id=1, source_target_pairs={{0,1},{1,0},{2,3},{3,2},{4,5},{5,4},{6,7},{7,6},{8,9},{9,8},{10,11... | collective-permute-start | bytes 393224 | tf_op jit(solution)/shard_map/ppermute | solution.py:570
  42.0 1.4 %collective-permute-start.2 = (f32[64,4,128]{2,1,0:T(4,128)S(1)}, f32[64,4,128]{2,1,0:T(4,128)S(1)}, u32[]{:S(2)}, u32[]{:S(2)}) collective-permute-start(f32[64,4,128]{2,1,0:T(4,128)S(1)} %get-tuple-element.24.mine_ref), channel_id=1, source_target_pairs={{0,1},{1,0},{2,3},{3,2},{4,5},{5,4},{6,7},{7,6},{8,9},{9,8},{10,11... | collective-permute-start | bytes 393224 | tf_op jit(solution)/shard_map/ppermute | solution.py:581

commit v6 on v5

--- a/solution.py
+++ b/solution.py
@@ -15,9 +15,9 @@
 nugget = 1.0
 tiles_per_step = 8
 rows_here = 4
-chunk_bits = 2
+chunk_bits = 1
 chunk = 1 << chunk_bits
-chunks_per_step = 40
+chunks_per_step = 135
 tile_bytes_limit = 24 * 2**20
 kernel_bytes = 12 * 2**20
 f32 = jnp.float32
@@ -165,7 +165,7 @@
 def tile_schedule(listed, blocks):
     half = (listed + 1) // 2
     entries = half + blocks // 2
-    sizes = range(20, 39)
+    sizes = range(40, 48)
     width = min(sizes, key=lambda size: (-(-entries // (2 * size)) * size, -size))
     steps = -(-entries // (2 * width)) * 2
     longest = (2 * half + blocks // 2 + 3 * blocks) // chunk
@@ -183,23 +183,24 @@
         copy.start()
     for copy in copies:
         copy.wait()
-    first = point_ref[:, 0:BLOCK]
-    second = point_ref[:, BLOCK : 2 * BLOCK]
-    first_high = first.astype(bf16).astype(f32)
-    second_high = second.astype(bf16).astype(f32)
-    for chip in range(devices // 2):
-        rows = pl.ds(chip * rows_here, rows_here)
-        parts = (
-            field_ref[rows, 0:BLOCK],
-            first_high,
-            field_ref[rows, BLOCK : 2 * BLOCK],
-            second_high,
-            second - second_high,
-            first - first_high,
-        )
-        message = jnp.concatenate(parts, axis=0).astype(bf16)
-        outgoing_ref[2 * chip] = message
-        outgoing_ref[2 * chip + 1] = message
+    row = row_number((8, BLOCK))
+    blank = jnp.zeros((4, BLOCK), f32)
+    high_parts, low_parts = [], []
+    for block in range(2):
+        points = point_ref[:, block * BLOCK : (block + 1) * BLOCK]
+        high = points.astype(bf16).astype(f32)
+        high_parts.append(jnp.concatenate([blank, high], axis=0))
+        low_parts.append(points - high)
+    low = jnp.concatenate([low_parts[1], low_parts[0]], axis=0)
+    for pair in range(devices // 4):
+        rows = pl.ds(8 * pair, 8)
+        fields = [field_ref[rows, block * BLOCK : (block + 1) * BLOCK] for block in range(2)]
+        turned = [pltpu.roll(field, 4, axis=0) for field in fields]
+        for side, chosen in enumerate((fields, turned)):
+            parts = [jnp.where(row < 4, chosen[block], high_parts[block]) for block in range(2)]
+            message = jnp.concatenate([*parts, low], axis=0).astype(bf16)
+            outgoing_ref[4 * pair + 2 * side] = message
+            outgoing_ref[4 * pair + 2 * side + 1] = message
 
 
 def listing_kernel(
@@ -309,12 +310,18 @@
     totals_ref[...] = jnp.zeros_like(totals_ref)
 
     def step(number, carry):
-        products = []
+        waiting = []
+
+        def add(item):
+            place, product = item
+            totals_ref[owner_ref[place]] += product
+
         for part in range(chunks_per_step):
+            place = number * chunks_per_step + part
             fields = []
             tiles = []
             for slot in range(chunk):
-                entry = entry_ref[(number * chunks_per_step + part) * chunk + slot]
+                entry = entry_ref[place * chunk + slot]
                 fields.append(fields_ref[entry & 65535])
                 tiles.append(tiles_ref[entry >> 16])
             product = jnp.dot(
@@ -322,9 +329,11 @@
                 jnp.concatenate(tiles, axis=0),
                 preferred_element_type=f32,
             )
-            products.append(product[0:8])
-        for part in range(chunks_per_step):
-            totals_ref[owner_ref[number * chunks_per_step + part]] += products[part]
+            waiting.append((place, product[0:8]))
+            if len(waiting) > 8:
+                add(waiting.pop(0))
+        for item in waiting:
+            add(item)
         return carry
 
     lax.fori_loop(0, (count + chunks_per_step - 1) // chunks_per_step, step, 0)
@@ -599,7 +608,7 @@
     blocks = point_data.shape[1] // BLOCK * devices
     _, width, steps, _ = tile_schedule(pair_list.shape[1], blocks)
     tile_bytes = 2 * width * steps * BLOCK * BLOCK * 2
-    paired = col_devices % 2 == 0 and blocks == 2 * devices
+    paired = devices % 4 == 0 and col_devices % 2 == 0 and blocks == 2 * devices
     if paired and right_side.shape[0] == rows_here * (devices // 2) and tile_bytes <= tile_bytes_limit:
         return by_realizations(point_data, right_side, pair_list)
     return by_points(point_data, right_side, pair_list)

time: 54.5 us -> 53.1 us (0.974)
  Pallas kernels: 27.7 us -> 26.5 us
    pallas_call x2, Pallas kernels: 7.43 us -> 6.12 us  [by_realizations(): pl.pallas_call(functools.partial(next_kernel, first), out_shape=(product_...]
where the time goes in v6:
time: 53.1 us; the launch traced here: 52.8 us
  Pallas kernels  26.5 us (50%)
  blocking collectives  9.67 us (18%)
  starting transfers between devices  8.84 us (17%)
  waiting for transfers between devices  6.41 us (12%)
  local copies, waits for them, and re-layouts  0.71 us (1%)
  between operations  0.7 us (1%)
    pallas_call x1, Pallas kernels, by_realizations(): pl.pallas_call(functools.partial(first_kernel, plan), out_shape=(pltpu.VM...  13.1 us
    all_to_all x1, blocking collectives, by_realizations(): received = lax.all_to_all(result, axes, 0, 0, tiled=True)  9.67 us
    all_to_all x1, starting transfers between devices, by_realizations(): received = lax.all_to_all(outgoing, axes, 0, 0, tiled=True)  7.3 us
    pallas_call x2, Pallas kernels, by_realizations(): pl.pallas_call(functools.partial(next_kernel, first), out_shape=(product_...  6.12 us
    pallas_call x1, Pallas kernels, by_realizations(): pl.pallas_call(functools.partial(listing_kernel, plan, blocks), out_shape...  5.42 us
    all_to_all x1, waiting for transfers between devices, by_realizations(): received = lax.all_to_all(outgoing, axes, 0, 0, tiled=True)  3.45 us
    ppermute x3, waiting for transfers between devices, by_realizations(): other = lax.ppermute(mine, 'col', swap)  2.96 us
    pallas_call x1, Pallas kernels, by_realizations(): pl.pallas_call(packing_kernel, out_shape=jax.ShapeDtypeStruct((devices, 2...  1.57 us
  transfers between devices with their start and end apart: 4, of which 4 were waited for; matrix products, arithmetic and copies ran while one was open for 0% of the time, Pallas kernels for 10%

profile of v6, /device:TPU:0, one launch (start us, length us, event | category | flops | bytes accessed | tf_op | source)
XLA Modules:
  0.0 52.8 jit_solution(14771267482261614977)
XLA Ops:
  0.6 1.6 %shard_map.51 = bf16[32,24,128]{2,1,0:T(8,128)(2,1)} custom-call(f32[4,256]{1,0:T(4,128)} %point_hbm.1, f32[64,256]{1,0:T(8,128)} %field_hbm.1), custom_call_target="tpu_custom_call" | custom-call | tf_op jit(solution)/shard_map/pallas_call | solution.py:521
  2.2 7.3 %all-to-all-start = ((bf16[32,24,128]{2,1,0:T(8,128)(2,1)}), bf16[32,24,128]{2,1,0:T(8,128)(2,1)S(1)}, u32[]{:S(2)}, u32[]{:S(2)}) async-start(bf16[32,24,128]{2,1,0:T(8,128)(2,1)} %shard_map.51), calls=%async_computation | async-start | bytes 393216 | tf_op jit(solution)/shard_map/all_to_all | solution.py:555
  9.5 5.4 %shard_map.50 = (s32[548]{0:T(1024)S(4)}, s32[1088]{0:T(1024)S(4)}, s32[1]{0:T(128)S(4)}, s32[270]{0:T(512)S(4)}, s32[270]{0:T(512)S(4)}) custom-call(s32[1]{0:T(128)} %bitcast.core_ref, s32[2,468]{1,0:T(2,128)} %pair_hbm.1), custom_call_target="tpu_custom_call" | custom-call | flops 8000000000 | bytes 20000000 | tf_op jit(solution)/shard_map/pallas_call | solution.py:536
  14.9 3.5 %all-to-all-done.received_ref = bf16[32,24,128]{2,1,0:T(8,128)(2,1)S(1)} async-done(((bf16[32,24,128]{2,1,0:T(8,128)(2,1)}), bf16[32,24,128]{2,1,0:T(8,128)(2,1)S(1)}, u32[]{:S(2)}, u32[]{:S(2)}) %all-to-all-start) | async-done | bytes 196640 | tf_op jit(solution)/shard_map/all_to_all | solution.py:555
  18.4 13.1 %shard_map.52 = (bf16[540,128,128]{2,1,0:T(8,128)(2,1)S(1)}, f32[64,4,128]{2,1,0:T(4,128)S(1)}, f32[64,8,128]{2,1,0:T(8,128)S(1)}) custom-call(s32[270]{0:T(512)S(4)} %get-tuple-element.14.low_ref, s32[270]{0:T(512)S(4)} %get-tuple-element.15.high_ref, bf16[32,24,128]{2,1,0:T(8,128)(2,1)S(1)} %all-to-all-done.received_ref), custom_call_target="tpu_custom_call" | custom-call | tf_op jit(solution)/shard_map/pallas_call | solution.py:562
  31.5 0.7 %collective-permute-start = (f32[64,4,128]{2,1,0:T(4,128)S(1)}, f32[64,4,128]{2,1,0:T(4,128)S(1)}, u32[]{:S(2)}, u32[]{:S(2)}) collective-permute-start(f32[64,4,128]{2,1,0:T(4,128)S(1)} %get-tuple-element.20.mine_ref), channel_id=1, source_target_pairs={{0,1},{1,0},{2,3},{3,2},{4,5},{5,4},{6,7},{7,6},{8,9},{9,8},{10,11... | collective-permute-start | bytes 393224 | tf_op jit(solution)/shard_map/ppermute | solution.py:579
  32.1 1.0 %collective-permute-done.other_ref = f32[64,4,128]{2,1,0:T(4,128)S(1)} collective-permute-done((f32[64,4,128]{2,1,0:T(4,128)S(1)}, f32[64,4,128]{2,1,0:T(4,128)S(1)}, u32[]{:S(2)}, u32[]{:S(2)}) %collective-permute-start) | collective-permute-done | bytes 131104 | tf_op jit(solution)/shard_map/ppermute | solution.py:579
  33.1 3.1 %shard_map.53 = (f32[64,4,128]{2,1,0:T(4,128)S(1)}, f32[3,64,4,128]{3,2,1,0:T(4,128)S(1)}) custom-call(s32[548]{0:T(1024)S(4)} %get-tuple-element.17.owner_ref, s32[1088]{0:T(1024)S(4)} %get-tuple-element.18.entry_ref, s32[1]{0:T(128)S(4)} %get-tuple-element.19.count_ref, f32[64,8,128]{2,1,0:T(8,128)S(1)} %get-tuple-element.16.gathered_ref, ...), custom_call_target="tpu_custom_call" | custom-call | tf_op jit(solution)/shard_map/pallas_call | solution.py:582
  36.2 0.4 collective-permute-start.1
  36.6 1.0 %collective-permute-done.1.other_ref = f32[64,4,128]{2,1,0:T(4,128)S(1)} collective-permute-done((f32[64,4,128]{2,1,0:T(4,128)S(1)}, f32[64,4,128]{2,1,0:T(4,128)S(1)}, u32[]{:S(2)}, u32[]{:S(2)}) %collective-permute-start.1) | collective-permute-done | bytes 131104 | tf_op jit(solution)/shard_map/ppermute | solution.py:579
  37.6 3.1 %shard_map.54 = (f32[64,4,128]{2,1,0:T(4,128)S(1)}, f32[3,64,4,128]{3,2,1,0:T(4,128)S(1)}) custom-call(s32[548]{0:T(1024)S(4)} %get-tuple-element.17.owner_ref, s32[1088]{0:T(1024)S(4)} %get-tuple-element.18.entry_ref, s32[1]{0:T(128)S(4)} %get-tuple-element.19.count_ref, f32[64,8,128]{2,1,0:T(8,128)S(1)} %get-tuple-element.16.gathered_ref, ...), custom_call_target="tpu_custom_call" | custom-call | tf_op jit(solution)/shard_map/pallas_call | solution.py:582
  40.7 0.4 collective-permute-start.2
  41.1 1.0 %collective-permute-done.2.other_ref = f32[64,4,128]{2,1,0:T(4,128)S(1)} collective-permute-done((f32[64,4,128]{2,1,0:T(4,128)S(1)}, f32[64,4,128]{2,1,0:T(4,128)S(1)}, u32[]{:S(2)}, u32[]{:S(2)}) %collective-permute-start.2) | collective-permute-done | bytes 131104 | tf_op jit(solution)/shard_map/ppermute | solution.py:590
  42.1 0.3 shard_map.55
  42.4 9.7 %all_to_all.10 = bf16[32,2,4,128]{3,2,1,0:T(4,128)(2,1)S(1)} all-to-all(bf16[32,2,4,128]{3,2,1,0:T(4,128)(2,1)S(1)} %bitcast.14), channel_id=1, replica_groups=mesh['row'=4,'col'=8] {'row','col'}, dimensions={0} | all-to-all | bytes 131072 | tf_op jit(solution)/shard_map/all_to_all | solution.py:599
  52.1 0.1 copy.11
  52.2 0.7 %copy_bitcast_fusion = (f32[64,256]{1,0:T(8,128)}, f32[64,256]{1,0:T(8,128)}) fusion(f32[8,8,2,128]{3,2,1,0:T(2,128)S(1)} %bitcast.16, f32[8,8,2,128]{3,2,1,0:T(2,128)S(1)} %bitcast.17), kind=kLoop, calls=%fused_computation | loop fusion | bytes 262144 | tf_op jit(solution)/shard_map/convert_element_type | solution.py:602
  (1 shorter events, 0.0 us)
Async XLA Ops:
  2.2 16.2 %all-to-all-start = ((bf16[32,24,128]{2,1,0:T(8,128)(2,1)}), bf16[32,24,128]{2,1,0:T(8,128)(2,1)S(1)}, u32[]{:S(2)}, u32[]{:S(2)}) async-start(bf16[32,24,128]{2,1,0:T(8,128)(2,1)} %shard_map.51), calls=%async_computation | async-start | bytes 393216 | tf_op jit(solution)/shard_map/all_to_all | solution.py:555
  31.5 1.7 %collective-permute-start = (f32[64,4,128]{2,1,0:T(4,128)S(1)}, f32[64,4,128]{2,1,0:T(4,128)S(1)}, u32[]{:S(2)}, u32[]{:S(2)}) collective-permute-start(f32[64,4,128]{2,1,0:T(4,128)S(1)} %get-tuple-element.20.mine_ref), channel_id=1, source_target_pairs={{0,1},{1,0},{2,3},{3,2},{4,5},{5,4},{6,7},{7,6},{8,9},{9,8},{10,11... | collective-permute-start | bytes 393224 | tf_op jit(solution)/shard_map/ppermute | solution.py:579
  36.2 1.4 %collective-permute-start.1 = (f32[64,4,128]{2,1,0:T(4,128)S(1)}, f32[64,4,128]{2,1,0:T(4,128)S(1)}, u32[]{:S(2)}, u32[]{:S(2)}) collective-permute-start(f32[64,4,128]{2,1,0:T(4,128)S(1)} %get-tuple-element.22.mine_ref), channel_id=1, source_target_pairs={{0,1},{1,0},{2,3},{3,2},{4,5},{5,4},{6,7},{7,6},{8,9},{9,8},{10,11... | collective-permute-start | bytes 393224 | tf_op jit(solution)/shard_map/ppermute | solution.py:579
  40.7 1.4 %collective-permute-start.2 = (f32[64,4,128]{2,1,0:T(4,128)S(1)}, f32[64,4,128]{2,1,0:T(4,128)S(1)}, u32[]{:S(2)}, u32[]{:S(2)}) collective-permute-start(f32[64,4,128]{2,1,0:T(4,128)S(1)} %get-tuple-element.24.mine_ref), channel_id=1, source_target_pairs={{0,1},{1,0},{2,3},{3,2},{4,5},{5,4},{6,7},{7,6},{8,9},{9,8},{10,11... | collective-permute-start | bytes 393224 | tf_op jit(solution)/shard_map/ppermute | solution.py:590

commit v7 on v6

--- a/solution.py
+++ b/solution.py
@@ -279,7 +279,7 @@
     distance = squared * lax.rsqrt(squared)
     near = jnp.maximum(1.0 - distance * (1.0 / long_range), 0.0)
     near_square = near * near
-    wide = near_square * near_square * (1.25 - near)
+    wide = near_square * near_square * (0.25 + distance)
     close = jnp.asarray(1.0, bf16) - distance.astype(bf16) * jnp.asarray(1.0 / short_range, bf16)
     close = jnp.maximum(close, jnp.asarray(0.0, bf16))
     close_square = close * close
@@ -500,7 +500,22 @@
     scale = gathered_ref[:, 7:8, :]
     moved, residual, _ = advance(mine_ref, other_ref, scale, state_ref[2], state_ref[1])
     chosen = jnp.where(core_ref[0] == 0, state_ref[0] + moved, residual)
-    result_ref[...] = chosen.astype(bf16)
+    for device in range(result_ref.shape[0]):
+        both = jnp.concatenate([chosen[2 * device], chosen[2 * device + 1]], axis=0)
+        result_ref[device] = both.astype(bf16)
+
+
+def unpacking_kernel(received_ref, solution_ref, residual_ref):
+    row = row_number((8, BLOCK))
+    for pair in range(received_ref.shape[0] // 4):
+        for side, output_ref in enumerate((solution_ref, residual_ref)):
+            even = received_ref[4 * pair + side].astype(f32)
+            odd = received_ref[4 * pair + 2 + side].astype(f32)
+            rows = pl.ds(8 * pair, 8)
+            turned = pltpu.roll(odd, 4, axis=0)
+            output_ref[rows, 0:BLOCK] = jnp.where(row < 4, even, turned)
+            turned = pltpu.roll(even, 4, axis=0)
+            output_ref[rows, BLOCK : 2 * BLOCK] = jnp.where(row < 4, turned, odd)
 
 
 def by_realizations(point_data, right_side, pair_list):
@@ -590,16 +605,20 @@
     other = lax.ppermute(mine, "col", swap)
     result = pl.pallas_call(
         last_kernel,
-        out_shape=jax.ShapeDtypeStruct((blocks, rows_here, BLOCK), bf16),
+        out_shape=jax.ShapeDtypeStruct((devices, 2 * rows_here, BLOCK), bf16),
         in_specs=[scalar] + [vector] * 4,
         out_specs=vector,
         compiler_params=limits,
     )(core, gathered, mine, other, state)
-    result = result.reshape(devices, blocks_here, rows_here, BLOCK)
     received = lax.all_to_all(result, axes, 0, 0, tiled=True)
-    received = received.reshape(chips, 2, blocks_here, rows_here, BLOCK)
-    received = received.transpose(1, 0, 3, 2, 4).reshape(2, right_side.shape[0], -1)
-    return received[0].astype(f32), received[1].astype(f32)
+    output_shape = jax.ShapeDtypeStruct(right_side.shape, f32)
+    return pl.pallas_call(
+        unpacking_kernel,
+        out_shape=(output_shape, output_shape),
+        in_specs=[vector],
+        out_specs=(vector, vector),
+        compiler_params=limits,
+    )(received)
 
 
 def per_device(point_data, right_side, pair_list):

time: 53.1 us -> 53.1 us (level)
  local copies, waits for them, and re-layouts: 0.71 us -> 0 us
  Pallas kernels: 26.5 us -> 27.2 us
    pallas_call x1 -> x2, Pallas kernels: 0.29 us -> 0.95 us  [the longest x1 0.67 us: by_realizations(): pl.pallas_call(unpacking_kernel, out_shape=(output_shape, output_shape),...]
    convert_element_type x1 -> x0, local copies, waits for them, and re-layouts: 0.66 us -> none  [by_realizations(): return (received[0].astype(f32), received[1].astype(f32))]
where the time goes in v7:
time: 53.1 us; the launch traced here: 52.8 us
  Pallas kernels  27.2 us (51%)
  blocking collectives  9.69 us (18%)
  starting transfers between devices  8.82 us (17%)
  waiting for transfers between devices  6.42 us (12%)
  between operations  0.69 us (1%)
    pallas_call x1, Pallas kernels, by_realizations(): pl.pallas_call(functools.partial(first_kernel, plan), out_shape=(pltpu.VM...  13.1 us
    all_to_all x1, blocking collectives, by_realizations(): received = lax.all_to_all(result, axes, 0, 0, tiled=True)  9.69 us
    all_to_all x1, starting transfers between devices, by_realizations(): received = lax.all_to_all(outgoing, axes, 0, 0, tiled=True)  7.3 us
    pallas_call x2, Pallas kernels, by_realizations(): pl.pallas_call(functools.partial(next_kernel, first), out_shape=(product_...  6.13 us
    pallas_call x1, Pallas kernels, by_realizations(): pl.pallas_call(functools.partial(listing_kernel, plan, blocks), out_shape...  5.42 us
    all_to_all x1, waiting for transfers between devices, by_realizations(): received = lax.all_to_all(outgoing, axes, 0, 0, tiled=True)  3.45 us
    ppermute x3, waiting for transfers between devices, by_realizations(): other = lax.ppermute(mine, 'col', swap)  2.97 us
    pallas_call x1, Pallas kernels, by_realizations(): pl.pallas_call(packing_kernel, out_shape=jax.ShapeDtypeStruct((devices, 2...  1.56 us
  transfers between devices with their start and end apart: 4, of which 4 were waited for; matrix products, arithmetic and copies ran while one was open for 0% of the time, Pallas kernels for 10%

profile of v7, /device:TPU:0, one launch (start us, length us, event | category | flops | bytes accessed | tf_op | source)
XLA Modules:
  0.0 52.8 jit_solution(6752082826242486469)
XLA Ops:
  0.6 1.6 %shard_map.51 = bf16[32,24,128]{2,1,0:T(8,128)(2,1)} custom-call(f32[4,256]{1,0:T(4,128)} %point_hbm.1, f32[64,256]{1,0:T(8,128)} %field_hbm.1), custom_call_target="tpu_custom_call" | custom-call | tf_op jit(solution)/shard_map/pallas_call | solution.py:536
  2.2 7.3 %all-to-all-start = ((bf16[32,24,128]{2,1,0:T(8,128)(2,1)}), bf16[32,24,128]{2,1,0:T(8,128)(2,1)S(1)}, u32[]{:S(2)}, u32[]{:S(2)}) async-start(bf16[32,24,128]{2,1,0:T(8,128)(2,1)} %shard_map.51), calls=%async_computation | async-start | bytes 393216 | tf_op jit(solution)/shard_map/all_to_all | solution.py:570
  9.5 5.4 %shard_map.50 = (s32[548]{0:T(1024)S(4)}, s32[1088]{0:T(1024)S(4)}, s32[1]{0:T(128)S(4)}, s32[270]{0:T(512)S(4)}, s32[270]{0:T(512)S(4)}) custom-call(s32[1]{0:T(128)} %bitcast.core_ref, s32[2,468]{1,0:T(2,128)} %pair_hbm.1), custom_call_target="tpu_custom_call" | custom-call | flops 8000000000 | bytes 20000000 | tf_op jit(solution)/shard_map/pallas_call | solution.py:551
  14.9 3.5 %all-to-all-done.received_ref = bf16[32,24,128]{2,1,0:T(8,128)(2,1)S(1)} async-done(((bf16[32,24,128]{2,1,0:T(8,128)(2,1)}), bf16[32,24,128]{2,1,0:T(8,128)(2,1)S(1)}, u32[]{:S(2)}, u32[]{:S(2)}) %all-to-all-start) | async-done | bytes 196640 | tf_op jit(solution)/shard_map/all_to_all | solution.py:570
  18.4 13.1 %shard_map.52 = (bf16[540,128,128]{2,1,0:T(8,128)(2,1)S(1)}, f32[64,4,128]{2,1,0:T(4,128)S(1)}, f32[64,8,128]{2,1,0:T(8,128)S(1)}) custom-call(s32[270]{0:T(512)S(4)} %get-tuple-element.14.low_ref, s32[270]{0:T(512)S(4)} %get-tuple-element.15.high_ref, bf16[32,24,128]{2,1,0:T(8,128)(2,1)S(1)} %all-to-all-done.received_ref), custom_call_target="tpu_custom_call" | custom-call | tf_op jit(solution)/shard_map/pallas_call | solution.py:577
  31.5 0.7 %collective-permute-start = (f32[64,4,128]{2,1,0:T(4,128)S(1)}, f32[64,4,128]{2,1,0:T(4,128)S(1)}, u32[]{:S(2)}, u32[]{:S(2)}) collective-permute-start(f32[64,4,128]{2,1,0:T(4,128)S(1)} %get-tuple-element.20.mine_ref), channel_id=1, source_target_pairs={{0,1},{1,0},{2,3},{3,2},{4,5},{5,4},{6,7},{7,6},{8,9},{9,8},{10,11... | collective-permute-start | bytes 393224 | tf_op jit(solution)/shard_map/ppermute | solution.py:594
  32.2 1.0 %collective-permute-done.other_ref = f32[64,4,128]{2,1,0:T(4,128)S(1)} collective-permute-done((f32[64,4,128]{2,1,0:T(4,128)S(1)}, f32[64,4,128]{2,1,0:T(4,128)S(1)}, u32[]{:S(2)}, u32[]{:S(2)}) %collective-permute-start) | collective-permute-done | bytes 131104 | tf_op jit(solution)/shard_map/ppermute | solution.py:594
  33.2 3.1 %shard_map.53 = (f32[64,4,128]{2,1,0:T(4,128)S(1)}, f32[3,64,4,128]{3,2,1,0:T(4,128)S(1)}) custom-call(s32[548]{0:T(1024)S(4)} %get-tuple-element.17.owner_ref, s32[1088]{0:T(1024)S(4)} %get-tuple-element.18.entry_ref, s32[1]{0:T(128)S(4)} %get-tuple-element.19.count_ref, f32[64,8,128]{2,1,0:T(8,128)S(1)} %get-tuple-element.16.gathered_ref, ...), custom_call_target="tpu_custom_call" | custom-call | tf_op jit(solution)/shard_map/pallas_call | solution.py:597
  36.2 0.4 collective-permute-start.1
  36.7 1.0 %collective-permute-done.1.other_ref = f32[64,4,128]{2,1,0:T(4,128)S(1)} collective-permute-done((f32[64,4,128]{2,1,0:T(4,128)S(1)}, f32[64,4,128]{2,1,0:T(4,128)S(1)}, u32[]{:S(2)}, u32[]{:S(2)}) %collective-permute-start.1) | collective-permute-done | bytes 131104 | tf_op jit(solution)/shard_map/ppermute | solution.py:594
  37.6 3.1 %shard_map.54 = (f32[64,4,128]{2,1,0:T(4,128)S(1)}, f32[3,64,4,128]{3,2,1,0:T(4,128)S(1)}) custom-call(s32[548]{0:T(1024)S(4)} %get-tuple-element.17.owner_ref, s32[1088]{0:T(1024)S(4)} %get-tuple-element.18.entry_ref, s32[1]{0:T(128)S(4)} %get-tuple-element.19.count_ref, f32[64,8,128]{2,1,0:T(8,128)S(1)} %get-tuple-element.16.gathered_ref, ...), custom_call_target="tpu_custom_call" | custom-call | tf_op jit(solution)/shard_map/pallas_call | solution.py:597
  40.7 0.4 collective-permute-start.2
  41.1 1.0 %collective-permute-done.2.other_ref = f32[64,4,128]{2,1,0:T(4,128)S(1)} collective-permute-done((f32[64,4,128]{2,1,0:T(4,128)S(1)}, f32[64,4,128]{2,1,0:T(4,128)S(1)}, u32[]{:S(2)}, u32[]{:S(2)}) %collective-permute-start.2) | collective-permute-done | bytes 131104 | tf_op jit(solution)/shard_map/ppermute | solution.py:605
  42.1 0.3 shard_map.55
  42.4 9.7 %all_to_all.10.received_ref = bf16[32,8,128]{2,1,0:T(8,128)(2,1)S(1)} all-to-all(bf16[32,8,128]{2,1,0:T(8,128)(2,1)S(1)} %shard_map.55), channel_id=1, replica_groups=mesh['row'=4,'col'=8] {'row','col'}, dimensions={0} | all-to-all | bytes 131072 | tf_op jit(solution)/shard_map/all_to_all | solution.py:613
  52.1 0.7 %shard_map.56 = (f32[64,256]{1,0:T(8,128)}, f32[64,256]{1,0:T(8,128)}) custom-call(bf16[32,8,128]{2,1,0:T(8,128)(2,1)S(1)} %all_to_all.10.received_ref), custom_call_target="tpu_custom_call" | custom-call | tf_op jit(solution)/shard_map/pallas_call | solution.py:615
Async XLA Ops:
  2.2 16.2 %all-to-all-start = ((bf16[32,24,128]{2,1,0:T(8,128)(2,1)}), bf16[32,24,128]{2,1,0:T(8,128)(2,1)S(1)}, u32[]{:S(2)}, u32[]{:S(2)}) async-start(bf16[32,24,128]{2,1,0:T(8,128)(2,1)} %shard_map.51), calls=%async_computation | async-start | bytes 393216 | tf_op jit(solution)/shard_map/all_to_all | solution.py:570
  31.5 1.7 %collective-permute-start = (f32[64,4,128]{2,1,0:T(4,128)S(1)}, f32[64,4,128]{2,1,0:T(4,128)S(1)}, u32[]{:S(2)}, u32[]{:S(2)}) collective-permute-start(f32[64,4,128]{2,1,0:T(4,128)S(1)} %get-tuple-element.20.mine_ref), channel_id=1, source_target_pairs={{0,1},{1,0},{2,3},{3,2},{4,5},{5,4},{6,7},{7,6},{8,9},{9,8},{10,11... | collective-permute-start | bytes 393224 | tf_op jit(solution)/shard_map/ppermute | solution.py:594
  36.2 1.4 %collective-permute-start.1 = (f32[64,4,128]{2,1,0:T(4,128)S(1)}, f32[64,4,128]{2,1,0:T(4,128)S(1)}, u32[]{:S(2)}, u32[]{:S(2)}) collective-permute-start(f32[64,4,128]{2,1,0:T(4,128)S(1)} %get-tuple-element.22.mine_ref), channel_id=1, source_target_pairs={{0,1},{1,0},{2,3},{3,2},{4,5},{5,4},{6,7},{7,6},{8,9},{9,8},{10,11... | collective-permute-start | bytes 393224 | tf_op jit(solution)/shard_map/ppermute | solution.py:594
  40.7 1.4 %collective-permute-start.2 = (f32[64,4,128]{2,1,0:T(4,128)S(1)}, f32[64,4,128]{2,1,0:T(4,128)S(1)}, u32[]{:S(2)}, u32[]{:S(2)}) collective-permute-start(f32[64,4,128]{2,1,0:T(4,128)S(1)} %get-tuple-element.24.mine_ref), channel_id=1, source_target_pairs={{0,1},{1,0},{2,3},{3,2},{4,5},{5,4},{6,7},{7,6},{8,9},{9,8},{10,11... | collective-permute-start | bytes 393224 | tf_op jit(solution)/shard_map/ppermute | solution.py:605

commit v8 on v6

--- a/solution.py
+++ b/solution.py
@@ -165,10 +165,10 @@
 def tile_schedule(listed, blocks):
     half = (listed + 1) // 2
     entries = half + blocks // 2
-    sizes = range(40, 48)
+    sizes = range(64, 70)
     width = min(sizes, key=lambda size: (-(-entries // (2 * size)) * size, -size))
     steps = -(-entries // (2 * width)) * 2
-    longest = (2 * half + blocks // 2 + 3 * blocks) // chunk
+    longest = (2 * half + blocks // 2 + (chunk - 1) * blocks) // chunk
     chunks = -(-longest // chunks_per_step) * chunks_per_step + chunks_per_step
     return half, width, steps, chunks
 
@@ -228,18 +228,15 @@
         open_ref[block] = 0
         return carry
 
-    def pad(place, carry):
-        entry_ref[place] = blocks
-        return carry
-
     lax.fori_loop(0, blocks, clear, 0, unroll=16)
-    lax.fori_loop(0, chunks * chunk, pad, 0, unroll=16)
 
     def append(block, entry, used):
         place = open_ref[block]
         fresh = (place & (chunk - 1)) == 0
         place = jnp.where(fresh, used, place)
         open_ref[block] = place + 1
+        for slot in range(1, chunk):
+            entry_ref[place | slot] = blocks
         entry_ref[place] = entry
         owner_ref[place >> chunk_bits] = block
         return jnp.where(fresh, used + chunk, used)
@@ -272,6 +269,8 @@
     count_ref[0] = used
     for part in range(chunks_per_step):
         owner_ref[used + part] = blocks
+        for slot in range(chunk):
+            entry_ref[(used + part) * chunk + slot] = blocks
 
 
 def radial(squared):

time: 53.1 us -> 53.3 us (level)
  no operation moved by 1% of the time
where the time goes in v8:
time: 53.3 us; the launch traced here: 53 us
  Pallas kernels  26.5 us (50%)
  blocking collectives  9.7 us (18%)
  starting transfers between devices  8.81 us (17%)
  waiting for transfers between devices  6.49 us (12%)
  local copies, waits for them, and re-layouts  0.71 us (1%)
  between operations  0.7 us (1%)
    pallas_call x1, Pallas kernels, by_realizations(): pl.pallas_call(functools.partial(first_kernel, plan), out_shape=(pltpu.VM...  13.2 us
    all_to_all x1, blocking collectives, by_realizations(): received = lax.all_to_all(result, axes, 0, 0, tiled=True)  9.7 us
    all_to_all x1, starting transfers between devices, by_realizations(): received = lax.all_to_all(outgoing, axes, 0, 0, tiled=True)  7.3 us
    pallas_call x2, Pallas kernels, by_realizations(): pl.pallas_call(functools.partial(next_kernel, first), out_shape=(product_...  6.13 us
    pallas_call x1, Pallas kernels, by_realizations(): pl.pallas_call(functools.partial(listing_kernel, plan, blocks), out_shape...  5.35 us
    all_to_all x1, waiting for transfers between devices, by_realizations(): received = lax.all_to_all(outgoing, axes, 0, 0, tiled=True)  3.52 us
    ppermute x3, waiting for transfers between devices, by_realizations(): other = lax.ppermute(mine, 'col', swap)  2.97 us
    pallas_call x1, Pallas kernels, by_realizations(): pl.pallas_call(packing_kernel, out_shape=jax.ShapeDtypeStruct((devices, 2...  1.57 us
  transfers between devices with their start and end apart: 4, of which 4 were waited for; matrix products, arithmetic and copies ran while one was open for 0% of the time, Pallas kernels for 10%

profile of v8, /device:TPU:0, one launch (start us, length us, event | category | flops | bytes accessed | tf_op | source)
XLA Modules:
  0.0 53.0 jit_solution(15169078249044473537)
XLA Ops:
  0.6 1.6 %shard_map.51 = bf16[32,24,128]{2,1,0:T(8,128)(2,1)} custom-call(f32[4,256]{1,0:T(4,128)} %point_hbm.1, f32[64,256]{1,0:T(8,128)} %field_hbm.1), custom_call_target="tpu_custom_call" | custom-call | tf_op jit(solution)/shard_map/pallas_call | solution.py:520
  2.2 7.3 %all-to-all-start = ((bf16[32,24,128]{2,1,0:T(8,128)(2,1)}), bf16[32,24,128]{2,1,0:T(8,128)(2,1)S(1)}, u32[]{:S(2)}, u32[]{:S(2)}) async-start(bf16[32,24,128]{2,1,0:T(8,128)(2,1)} %shard_map.51), calls=%async_computation | async-start | bytes 393216 | tf_op jit(solution)/shard_map/all_to_all | solution.py:554
  9.5 5.4 %shard_map.50 = (s32[548]{0:T(1024)S(4)}, s32[1088]{0:T(1024)S(4)}, s32[1]{0:T(128)S(4)}, s32[268]{0:T(512)S(4)}, s32[268]{0:T(512)S(4)}) custom-call(s32[1]{0:T(128)} %bitcast.core_ref, s32[2,468]{1,0:T(2,128)} %pair_hbm.1), custom_call_target="tpu_custom_call" | custom-call | flops 8000000000 | bytes 20000000 | tf_op jit(solution)/shard_map/pallas_call | solution.py:535
  14.9 3.5 %all-to-all-done.received_ref = bf16[32,24,128]{2,1,0:T(8,128)(2,1)S(1)} async-done(((bf16[32,24,128]{2,1,0:T(8,128)(2,1)}), bf16[32,24,128]{2,1,0:T(8,128)(2,1)S(1)}, u32[]{:S(2)}, u32[]{:S(2)}) %all-to-all-start) | async-done | bytes 196640 | tf_op jit(solution)/shard_map/all_to_all | solution.py:554
  18.4 13.2 %shard_map.52 = (bf16[536,128,128]{2,1,0:T(8,128)(2,1)S(1)}, f32[64,4,128]{2,1,0:T(4,128)S(1)}, f32[64,8,128]{2,1,0:T(8,128)S(1)}) custom-call(s32[268]{0:T(512)S(4)} %get-tuple-element.14.low_ref, s32[268]{0:T(512)S(4)} %get-tuple-element.15.high_ref, bf16[32,24,128]{2,1,0:T(8,128)(2,1)S(1)} %all-to-all-done.received_ref), custom_call_target="tpu_custom_call" | custom-call | tf_op jit(solution)/shard_map/pallas_call | solution.py:561
  31.6 0.7 %collective-permute-start = (f32[64,4,128]{2,1,0:T(4,128)S(1)}, f32[64,4,128]{2,1,0:T(4,128)S(1)}, u32[]{:S(2)}, u32[]{:S(2)}) collective-permute-start(f32[64,4,128]{2,1,0:T(4,128)S(1)} %get-tuple-element.20.mine_ref), channel_id=1, source_target_pairs={{0,1},{1,0},{2,3},{3,2},{4,5},{5,4},{6,7},{7,6},{8,9},{9,8},{10,11... | collective-permute-start | bytes 393224 | tf_op jit(solution)/shard_map/ppermute | solution.py:578
  32.2 1.0 %collective-permute-done.other_ref = f32[64,4,128]{2,1,0:T(4,128)S(1)} collective-permute-done((f32[64,4,128]{2,1,0:T(4,128)S(1)}, f32[64,4,128]{2,1,0:T(4,128)S(1)}, u32[]{:S(2)}, u32[]{:S(2)}) %collective-permute-start) | collective-permute-done | bytes 131104 | tf_op jit(solution)/shard_map/ppermute | solution.py:578
  33.2 3.1 %shard_map.53 = (f32[64,4,128]{2,1,0:T(4,128)S(1)}, f32[3,64,4,128]{3,2,1,0:T(4,128)S(1)}) custom-call(s32[548]{0:T(1024)S(4)} %get-tuple-element.17.owner_ref, s32[1088]{0:T(1024)S(4)} %get-tuple-element.18.entry_ref, s32[1]{0:T(128)S(4)} %get-tuple-element.19.count_ref, f32[64,8,128]{2,1,0:T(8,128)S(1)} %get-tuple-element.16.gathered_ref, ...), custom_call_target="tpu_custom_call" | custom-call | tf_op jit(solution)/shard_map/pallas_call | solution.py:581
  36.3 0.4 collective-permute-start.1
  36.7 1.0 %collective-permute-done.1.other_ref = f32[64,4,128]{2,1,0:T(4,128)S(1)} collective-permute-done((f32[64,4,128]{2,1,0:T(4,128)S(1)}, f32[64,4,128]{2,1,0:T(4,128)S(1)}, u32[]{:S(2)}, u32[]{:S(2)}) %collective-permute-start.1) | collective-permute-done | bytes 131104 | tf_op jit(solution)/shard_map/ppermute | solution.py:578
  37.7 3.1 %shard_map.54 = (f32[64,4,128]{2,1,0:T(4,128)S(1)}, f32[3,64,4,128]{3,2,1,0:T(4,128)S(1)}) custom-call(s32[548]{0:T(1024)S(4)} %get-tuple-element.17.owner_ref, s32[1088]{0:T(1024)S(4)} %get-tuple-element.18.entry_ref, s32[1]{0:T(128)S(4)} %get-tuple-element.19.count_ref, f32[64,8,128]{2,1,0:T(8,128)S(1)} %get-tuple-element.16.gathered_ref, ...), custom_call_target="tpu_custom_call" | custom-call | tf_op jit(solution)/shard_map/pallas_call | solution.py:581
  40.8 0.4 collective-permute-start.2
  41.2 1.0 %collective-permute-done.2.other_ref = f32[64,4,128]{2,1,0:T(4,128)S(1)} collective-permute-done((f32[64,4,128]{2,1,0:T(4,128)S(1)}, f32[64,4,128]{2,1,0:T(4,128)S(1)}, u32[]{:S(2)}, u32[]{:S(2)}) %collective-permute-start.2) | collective-permute-done | bytes 131104 | tf_op jit(solution)/shard_map/ppermute | solution.py:589
  42.2 0.3 shard_map.55
  42.5 9.7 %all_to_all.10 = bf16[32,2,4,128]{3,2,1,0:T(4,128)(2,1)S(1)} all-to-all(bf16[32,2,4,128]{3,2,1,0:T(4,128)(2,1)S(1)} %bitcast.14), channel_id=1, replica_groups=mesh['row'=4,'col'=8] {'row','col'}, dimensions={0} | all-to-all | bytes 131072 | tf_op jit(solution)/shard_map/all_to_all | solution.py:598
  52.2 0.1 copy.11
  52.3 0.7 %copy_bitcast_fusion = (f32[64,256]{1,0:T(8,128)}, f32[64,256]{1,0:T(8,128)}) fusion(f32[8,8,2,128]{3,2,1,0:T(2,128)S(1)} %bitcast.16, f32[8,8,2,128]{3,2,1,0:T(2,128)S(1)} %bitcast.17), kind=kLoop, calls=%fused_computation | loop fusion | bytes 262144 | tf_op jit(solution)/shard_map/convert_element_type | solution.py:601
  (1 shorter events, 0.0 us)
Async XLA Ops:
  2.2 16.2 %all-to-all-start = ((bf16[32,24,128]{2,1,0:T(8,128)(2,1)}), bf16[32,24,128]{2,1,0:T(8,128)(2,1)S(1)}, u32[]{:S(2)}, u32[]{:S(2)}) async-start(bf16[32,24,128]{2,1,0:T(8,128)(2,1)} %shard_map.51), calls=%async_computation | async-start | bytes 393216 | tf_op jit(solution)/shard_map/all_to_all | solution.py:554
  31.6 1.6 %collective-permute-start = (f32[64,4,128]{2,1,0:T(4,128)S(1)}, f32[64,4,128]{2,1,0:T(4,128)S(1)}, u32[]{:S(2)}, u32[]{:S(2)}) collective-permute-start(f32[64,4,128]{2,1,0:T(4,128)S(1)} %get-tuple-element.20.mine_ref), channel_id=1, source_target_pairs={{0,1},{1,0},{2,3},{3,2},{4,5},{5,4},{6,7},{7,6},{8,9},{9,8},{10,11... | collective-permute-start | bytes 393224 | tf_op jit(solution)/shard_map/ppermute | solution.py:578
  36.3 1.4 %collective-permute-start.1 = (f32[64,4,128]{2,1,0:T(4,128)S(1)}, f32[64,4,128]{2,1,0:T(4,128)S(1)}, u32[]{:S(2)}, u32[]{:S(2)}) collective-permute-start(f32[64,4,128]{2,1,0:T(4,128)S(1)} %get-tuple-element.22.mine_ref), channel_id=1, source_target_pairs={{0,1},{1,0},{2,3},{3,2},{4,5},{5,4},{6,7},{7,6},{8,9},{9,8},{10,11... | collective-permute-start | bytes 393224 | tf_op jit(solution)/shard_map/ppermute | solution.py:578
  40.8 1.4 %collective-permute-start.2 = (f32[64,4,128]{2,1,0:T(4,128)S(1)}, f32[64,4,128]{2,1,0:T(4,128)S(1)}, u32[]{:S(2)}, u32[]{:S(2)}) collective-permute-start(f32[64,4,128]{2,1,0:T(4,128)S(1)} %get-tuple-element.24.mine_ref), channel_id=1, source_target_pairs={{0,1},{1,0},{2,3},{3,2},{4,5},{5,4},{6,7},{7,6},{8,9},{9,8},{10,11... | collective-permute-start | bytes 393224 | tf_op jit(solution)/shard_map/ppermute | solution.py:589
